TPU v7x, 128 devices: a whole 4x4x4 slice. The times are simulated.
128 devices in a mesh: dp: 8 (over y, z_lo), seq: 16 (over x, z_hi, core).
Axes of the slice: x: 4, y: 4, z: 4 (z_hi: 2, z_lo: 2; z = z_hi * 2 + z_lo), core: 2. Of those that a mesh axis runs over, the one named last changes fastest.
Arguments:
- query_space: bfloat16 [8, 4096, 1536], P('dp', 'seq'), may hold values from -40 to 40
- key_space: bfloat16 [8, 4096, 1536], P('dp', 'seq'), may hold values from -40 to 40
- value_space: bfloat16 [8, 4096, 1536], P('dp', 'seq'), may hold values from -6 to 6
- query_time: bfloat16 [8, 4096, 1536], P('dp', 'seq'), may hold values from -40 to 40
- key_time: bfloat16 [8, 4096, 1536], P('dp', 'seq'), may hold values from -40 to 40
- upstream: bfloat16 [8, 4096, 3072], P('dp', 'seq'), may hold values from -6 to 6
- out_weight: bfloat16 [1536, 3072], replicated, may hold values from -0.15625 to 0.15625
- tile_mask: int32 [16, 16], replicated, may hold values from 0 to 1, as said below
Outputs:
- query_space_grad: bfloat16 [8, 4096, 1536], P('dp', 'seq')
- key_space_grad: bfloat16 [8, 4096, 1536], P('dp', 'seq')
- value_space_grad: bfloat16 [8, 4096, 1536], P('dp', 'seq')
- query_time_grad: bfloat16 [8, 4096, 1536], P('dp', 'seq')
- key_time_grad: bfloat16 [8, 4096, 1536], P('dp', 'seq')
- weight_grad: float32 [1536, 3072], P('seq')
Inputs may be any that keep to these rules, and one draw needn't show every extreme that they name: `tile_mask`: entry (i, i) is 1 for every tile i.
All inputs are finite; a program needn't handle non-finite values.
Results may differ from a plain program's by a relative error of at most 0.023.
Values may be sent and summed in bfloat16 or wider, within the bound.
A program may use at most 192 MiB of HBM per device.

v0:
```python
import math

import jax
import jax.numpy as jnp
from jax import lax
from jax.experimental import pallas as pl
from jax.experimental.pallas import tpu as pltpu
from jax.sharding import PartitionSpec as P

HEADS = 12
HD = 128
HH = HEADS * HD
D = 3072
ROWS = 256
P_SIZE = 512
TILE = 32
NT = 16
FRAMES = 8
PIX = ROWS // FRAMES
HALF = PIX // 2
YS = 4
BLOCK = HH // YS
COLS = D // 8
OUT_ROWS = 96
GROUPS = 4
GH = HEADS // GROUPS
GC = GH * HD
WCH = 6
WROWS = HH // WCH
SCALE = 1.0 / math.sqrt(HD)
NEG = -1e30
MESH = pl.DeviceIdType.MESH
F32 = jnp.float32
B16 = jnp.bfloat16


def mm(a, b, ca, cb):
    return lax.dot_general(a, b, (((ca,), (cb,)), ((), ())), preferred_element_type=F32)


def kernel(
    qs, ks, vs, qt, kt, up, w, mask,
    sqg_o, skg_o, svg_o, tqg_o, tkg_o, wg_o,
    q_s, k_s, v_s, w_s, u_s, tq_r, tk_r, so_r, oc_r, sc_r, t_r,
    a_b, b_b, c_b, d_b, pw, tw, bias, tbias, tt, wgf, csend, crecv, rsend, rrecv, red,
    dk_f, dv_f, dk_x, dv_x, dk_r, dv_r, hop, t_f,
    ld, kv_ss, kv_rs, y_ss, y_rs, a2a_ss, a2a_rs, so_rs, sc_rs, t_rs, hop_ss, hop_rs,
    c_ss, c_rs, r_ss, r_rs, g_ss, g_rs, x_ss, x_rs, out_s,
):
    dp = lax.axis_index("dp")
    seq = lax.axis_index("seq")
    y, zl = dp // 2, dp % 2
    x, zh, core = seq // 4, (seq // 2) % 2, seq % 2
    frame = x * 2 + zh

    def dev(x_, y_, zh_, zl_, c_):
        return {"dp": y_ * 2 + zl_, "seq": x_ * 4 + zh_ * 2 + c_}

    def send(src, dst, ss, rs, to):
        pltpu.make_async_remote_copy(
            src_ref=src, dst_ref=dst, send_sem=ss, recv_sem=rs, device_id=to, device_id_type=MESH
        ).start()

    def await_bytes(ref, sem):
        pltpu.make_async_copy(ref, ref, sem).wait()

    def local(src, dst, sem):
        pltpu.make_async_copy(src, dst, sem).start()

    def rows(start, size):
        return pl.ds(pl.multiple_of(start, size), size)

    def spread(src, cols, put, unit, part):
        for zd in range(2):
            for side in range(2):
                far = ((x + 2) % 4 * 2 + zd) * PIX + side * HALF
                send(
                    src.at[rows(far, HALF), cols],
                    hop.at[unit, rows(side * PIX + zh * HALF, HALF), cols],
                    a2a_ss.at[unit], hop_rs.at[unit, part],
                    dev((x + 1 + 2 * side) % 4, y, zd, 1 - zl, core),
                )
        for step in (1, 3, 0):
            xd = (x + step) % 4
            for zd in range(2):
                put(
                    src, rows((xd * 2 + zd) * PIX, PIX), frame * PIX, PIX, a2a_ss.at[unit],
                    xd, zd, 1 - zl,
                )

    def forward(cols, put, unit, part):
        await_bytes(hop.at[unit, :, cols], hop_rs.at[unit, part])
        for side in range(2):
            came = (x + 3 + 2 * side) % 4
            for zs in range(2):
                put(
                    hop.at[unit], pl.ds(side * PIX + zs * HALF, HALF),
                    (came * 2 + zs) * PIX + side * HALF, HALF, hop_ss.at[unit],
                    (x + 1 + 2 * side) % 4, zh, zl,
                )

    def putter(dst, cols, rs):
        def put(src, src_rows, start, size, ss, xd, zd, zld):
            send(
                src.at[src_rows, cols], dst.at[rows(start, size), cols], ss, rs,
                dev(xd, y, zd, zld, core),
            )

        return put

    whole = pl.ds(0, HH)
    group_cols = [pl.ds(g * GC, GC) for g in range(GROUPS)]
    put_tq = putter(tq_r, whole, a2a_rs.at[0])
    put_tk = putter(tk_r, whole, a2a_rs.at[1])
    put_oc = putter(oc_r, whole, a2a_rs.at[2])
    put_so = [putter(so_r, group_cols[g], so_rs.at[g]) for g in range(GROUPS)]
    put_sc = [putter(sc_r, group_cols[g], sc_rs.at[g]) for g in range(GROUPS)]
    put_tqg = putter(tqg_o.at[0], whole, a2a_rs.at[5])
    put_tkg = putter(tkg_o.at[0], whole, a2a_rs.at[6])

    def put_out(src, src_rows, start, size, ss, xd, zd, zld):
        for k in range(YS):
            yd = (y + k) % YS
            send(
                src.at[src_rows, rows(yd * BLOCK, BLOCK)], t_r.at[rows(y * ROWS + start, size)],
                ss, t_rs, dev(xd, yd, zd, zld, core),
            )

    other = dev(x, y, zh, zl, 1 - core)
    y_up = dev(x, (y + 1) % YS, zh, zl, core)
    y_dn = dev(x, (y + 3) % YS, zh, zl, core)

    send(ks.at[0], k_s.at[pl.ds(ROWS, ROWS)], kv_ss.at[0], kv_rs.at[0], other)
    send(vs.at[0], v_s.at[pl.ds(ROWS, ROWS)], kv_ss.at[1], kv_rs.at[1], other)
    local(up.at[0], u_s.at[pl.ds(pl.multiple_of(y * ROWS, ROWS), ROWS)], ld.at[0])
    for i in range(WCH):
        local(w.at[pl.ds(i * WROWS, WROWS)], w_s.at[pl.ds(i * WROWS, WROWS)], ld.at[4 + i])
    local(qs.at[0], q_s, ld.at[1])
    local(ks.at[0], k_s.at[pl.ds(0, ROWS)], ld.at[2])
    local(vs.at[0], v_s.at[pl.ds(0, ROWS)], ld.at[3])
    half = ROWS // 2

    def u_half(owner, part):
        return u_s.at[pl.ds(pl.multiple_of(owner * ROWS + part * half, half), half)]

    send(up.at[0, pl.ds(0, half)], u_half(y, 0), y_ss.at[0], y_rs.at[0], y_up)
    send(up.at[0, pl.ds(half, half)], u_half(y, 1), y_ss.at[1], y_rs.at[1], y_dn)

    spread(qt.at[0], whole, put_tq, 0, 0)
    spread(kt.at[0], whole, put_tk, 1, 0)
    send(up.at[0, pl.ds(0, half)], u_half(y, 0), y_ss.at[2], y_rs.at[2], y_dn)
    send(up.at[0, pl.ds(half, half)], u_half(y, 1), y_ss.at[3], y_rs.at[3], y_up)

    key_row = lax.broadcasted_iota(jnp.int32, (P_SIZE, NT), 0)
    key_tile = jnp.where(
        key_row < ROWS, core * (NT // 2) + key_row // TILE,
        (1 - core) * (NT // 2) + (key_row - ROWS) // TILE,
    )
    key_hot = (key_tile == lax.broadcasted_iota(jnp.int32, (P_SIZE, NT), 1)).astype(F32)
    query_tile = core * (NT // 2) + lax.broadcasted_iota(jnp.int32, (ROWS, NT), 0) // TILE
    query_hot = (query_tile == lax.broadcasted_iota(jnp.int32, (ROWS, NT), 1)).astype(F32)
    rows_mask = mm(query_hot, mask[...].astype(F32), 1, 0)
    bias[...] = jnp.where(mm(key_hot, rows_mask, 1, 1) > 0.5, 0.0, NEG)
    same = (
        lax.broadcasted_iota(jnp.int32, (ROWS, ROWS), 0) % PIX
        == lax.broadcasted_iota(jnp.int32, (ROWS, ROWS), 1) % PIX
    )
    tbias[...] = jnp.where(same, 0.0, NEG)

    own_u = pl.ds(pl.multiple_of(y * ROWS, ROWS), ROWS)
    await_bytes(up.at[0], ld.at[0])

    for i in range(WCH):
        await_bytes(w_s.at[pl.ds(i * WROWS, WROWS)], ld.at[4 + i])
        c_b[:, pl.ds(i * WROWS, WROWS)] = mm(
            u_s[own_u, :], w_s[pl.ds(i * WROWS, WROWS), :], 1, 1
        ).astype(B16)

    forward(whole, put_tq, 0, 0)
    forward(whole, put_tk, 1, 0)

    await_bytes(q_s, ld.at[1])
    await_bytes(k_s.at[pl.ds(0, ROWS)], ld.at[2])
    await_bytes(v_s.at[pl.ds(0, ROWS)], ld.at[3])
    await_bytes(k_s.at[pl.ds(ROWS, ROWS)], kv_rs.at[0])
    await_bytes(v_s.at[pl.ds(ROWS, ROWS)], kv_rs.at[1])

    def space_forward(h, carry):
        hs = pl.ds(pl.multiple_of(h * HD, HD), HD)
        scores = mm(k_s[:, hs], q_s[:, hs], 1, 1) * SCALE + bias[...]
        powers = jnp.exp(scores - jnp.max(scores, axis=0, keepdims=True))
        weights = powers / jnp.sum(powers, axis=0, keepdims=True)
        pw[h] = weights
        a_b[:, hs] = mm(weights.astype(B16), v_s[:, hs], 0, 0).astype(B16)
        return carry

    for g in range(GROUPS):
        lax.fori_loop(g * GH, (g + 1) * GH, space_forward, 0)

        spread(a_b, group_cols[g], put_so[g], 3, g)

    spread(c_b, whole, put_oc, 2, 0)

    await_bytes(tq_r, a2a_rs.at[0])
    await_bytes(tk_r, a2a_rs.at[1])

    def time_forward(h, carry):
        hs = pl.ds(pl.multiple_of(h * HD, HD), HD)
        scores = mm(tk_r[:, hs], tq_r[:, hs], 1, 1) * SCALE + tbias[...]
        powers = jnp.exp(scores - jnp.max(scores, axis=0, keepdims=True))
        weights = powers / jnp.sum(powers, axis=0, keepdims=True)
        tw[h] = weights
        return carry

    lax.fori_loop(0, HEADS, time_forward, 0)
    for g in range(GROUPS):
        forward(group_cols[g], put_so[g], 3, g)

    y_m, y_p = (y + 3) % YS, (y + 1) % YS
    await_bytes(u_half(y_m, 0), y_rs.at[0])
    send(u_half(y_m, 0), u_half(y_m, 0), y_ss.at[4], y_rs.at[4], y_up)
    await_bytes(u_half(y_p, 1), y_rs.at[1])
    send(u_half(y_p, 1), u_half(y_p, 1), y_ss.at[5], y_rs.at[5], y_dn)

    for g in range(GROUPS):
        await_bytes(so_r.at[:, group_cols[g]], so_rs.at[g])
        heads = [
            mm(tw[h].astype(B16), so_r[:, h * HD:(h + 1) * HD], 0, 0)
            for h in range(g * GH, (g + 1) * GH)
        ]
        t_f[g] = jnp.concatenate(heads, axis=1)
    for k in range(YS):
        block = [t_f[g, :, k * OUT_ROWS:(k + 1) * OUT_ROWS] for g in range(GROUPS)]
        b_b[:, k * BLOCK:(k + 1) * BLOCK] = jnp.concatenate(block, axis=1).astype(B16)

    spread(b_b, whole, put_out, 7, 0)
    forward(whole, put_oc, 2, 0)

    await_bytes(oc_r, a2a_rs.at[2])
    await_bytes(c_b, a2a_ss.at[2])
    await_bytes(a_b, a2a_ss.at[3])

    def time_backward(h, carry):
        hs = pl.ds(pl.multiple_of(h * HD, HD), HD)
        weights = tw[h]
        cot = oc_r[:, hs]
        c_b[:, hs] = mm(weights.astype(B16), cot, 1, 0).astype(B16)
        prob = mm(so_r[:, hs], cot, 1, 1)
        centre = jnp.sum(weights * prob, axis=0, keepdims=True)
        grad = (weights * (prob - centre)).astype(B16)
        a_b[:, hs] = (mm(grad, tk_r[:, hs], 0, 0) * SCALE).astype(B16)
        d_b[:, hs] = (mm(grad, tq_r[:, hs], 1, 0) * SCALE).astype(B16)
        return carry

    for g in range(GROUPS):
        lax.fori_loop(g * GH, (g + 1) * GH, time_backward, 0)

        spread(c_b, group_cols[g], put_sc[g], 4, g)
        if g == 0:
            forward(whole, put_out, 7, 0)
        else:
            forward(group_cols[g - 1], put_sc[g - 1], 4, g - 1)

    forward(group_cols[GROUPS - 1], put_sc[GROUPS - 1], 4, GROUPS - 1)

    await_bytes(t_r, t_rs)
    tt[...] = t_r[...].T
    await_bytes(u_half(y_m, 1), y_rs.at[3])
    await_bytes(u_half(y_p, 0), y_rs.at[2])
    y_f = (y + 2) % YS
    await_bytes(u_half(y_f, 0), y_rs.at[4])
    await_bytes(u_half(y_f, 1), y_rs.at[5])

    def weight_part(chunk):
        return mm(tt[...], u_s[:, rows(chunk * COLS, COLS)], 1, 0)

    def pair_sum(i):
        await_bytes(crecv.at[i], c_rs.at[i])
        rsend[i] = (wgf[i] + crecv[i].astype(F32)).astype(B16)
        slot = rrecv.at[x * 4 + zh * 2 + zl]
        for k in range(4):
            xd = (x + k) % 4
            piece = rsend.at[i, rows(xd * OUT_ROWS, OUT_ROWS)]
            if k > 0:
                send(piece, slot, r_ss.at[k], r_rs, dev(xd, y, i // 2, i % 2, core))
            else:
                mine = zh * 2 + zl == i

                @pl.when(mine)
                def _():
                    local(piece, slot, r_rs)

                @pl.when(jnp.logical_not(mine))
                def _():
                    send(piece, slot, r_ss.at[0], r_rs, dev(xd, y, i // 2, i % 2, core))

    for i in range(4):
        csend[i] = weight_part(2 * i + 1 - core).astype(B16)
        send(csend.at[i], crecv.at[i], c_ss, c_rs.at[i], other)
        wgf[i] = weight_part(2 * i + core)
        if i > 0:
            pair_sum(i - 1)
    pair_sum(3)
    spread(a_b, whole, put_tqg, 5, 0)
    spread(d_b, whole, put_tkg, 6, 0)
    await_bytes(b_b, a2a_ss.at[7])

    def space_backward(h, carry):
        hs = pl.ds(pl.multiple_of(h * HD, HD), HD)
        weights = pw[h]
        cot = sc_r[:, hs]
        key = k_s[:, hs]
        prob = mm(v_s[:, hs], cot, 1, 1)
        centre = jnp.sum(weights * prob, axis=0, keepdims=True)
        grad = (weights * (prob - centre)).astype(B16)
        b_b[:, hs] = (mm(grad, key, 0, 0) * SCALE).astype(B16)
        dk = mm(grad, q_s[:, hs], 1, 0) * SCALE
        dv = mm(weights.astype(B16), cot, 1, 0)
        dk_f[:, hs] = dk[:ROWS]
        dv_f[:, hs] = dv[:ROWS]
        dk_x[:, hs] = dk[ROWS:].astype(B16)
        dv_x[:, hs] = dv[ROWS:].astype(B16)
        return carry

    def backward_group(g):
        cols = pl.ds(g * GC, GC)
        await_bytes(sc_r.at[:, cols], sc_rs.at[g])
        lax.fori_loop(g * GH, (g + 1) * GH, space_backward, 0)
        send(dk_x.at[:, cols], dk_r.at[:, cols], x_ss, x_rs.at[0, g], other)
        send(dv_x.at[:, cols], dv_r.at[:, cols], x_ss, x_rs.at[1, g], other)

    for g in range(GROUPS):
        backward_group(g)
        if g == 0:
            forward(whole, put_tqg, 5, 0)
            forward(whole, put_tkg, 6, 0)

    await_bytes(rrecv, r_rs)
    total = rrecv[0].astype(F32)
    for k in range(1, 16):
        total = total + rrecv[k].astype(F32)
    red[...] = total.astype(B16)
    out_cols = rows(((zh * 2 + zl) * 2 + core) * COLS, COLS)
    zh_own, core_own = y // 2, y % 2
    for k in range(8):
        yd, zld = (y + k // 2) % YS, (zl + k) % 2
        mine = (yd == y) & (zh_own == zh) & (zld == zl) & (core_own == core)

        @pl.when(mine)
        def _():
            local(red, wg_o.at[:, out_cols], g_rs)

        @pl.when(jnp.logical_not(mine))
        def _():
            send(red, wg_o.at[:, out_cols], g_ss.at[k], g_rs, dev(x, yd, zh_own, zld, core_own))

    local(b_b, sqg_o.at[0], out_s.at[0])
    for g in range(GROUPS):
        cols = pl.ds(g * GC, GC)
        await_bytes(dk_r.at[:, cols], x_rs.at[0, g])
        await_bytes(dv_r.at[:, cols], x_rs.at[1, g])
    await_bytes(dk_x, x_ss)
    await_bytes(dv_x, x_ss)
    dk_x[...] = (dk_f[...] + dk_r[...].astype(F32)).astype(B16)
    local(dk_x, skg_o.at[0], out_s.at[1])
    dv_x[...] = (dv_f[...] + dv_r[...].astype(F32)).astype(B16)
    local(dv_x, svg_o.at[0], out_s.at[2])

    await_bytes(ks.at[0], kv_ss.at[0])
    await_bytes(vs.at[0], kv_ss.at[1])
    for i in range(6):
        await_bytes(u_half(0, 0), y_ss.at[i])
    await_bytes(qt.at[0], a2a_ss.at[0])
    await_bytes(kt.at[0], a2a_ss.at[1])
    await_bytes(c_b, a2a_ss.at[4])
    await_bytes(a_b, a2a_ss.at[5])
    await_bytes(d_b, a2a_ss.at[6])
    for unit in range(8):
        await_bytes(hop.at[unit], hop_ss.at[unit])
    await_bytes(csend, c_ss)
    for k in range(1, 4):
        await_bytes(rsend.at[0], r_ss.at[k])
    await_bytes(rsend.at[0, pl.ds(0, 3 * OUT_ROWS)], r_ss.at[0])
    for k in range(8):
        yd, zld = (y + k // 2) % YS, (zl + k) % 2
        mine = (yd == y) & (zh_own == zh) & (zld == zl) & (core_own == core)

        @pl.when(jnp.logical_not(mine))
        def _():
            await_bytes(red, g_ss.at[k])

    await_bytes(tqg_o.at[0], a2a_rs.at[5])
    await_bytes(tkg_o.at[0], a2a_rs.at[6])
    await_bytes(wg_o, g_rs)
    await_bytes(b_b, out_s.at[0])
    await_bytes(dk_x, out_s.at[1])
    await_bytes(dv_x, out_s.at[2])


def local(qs, ks, vs, qt, kt, up, w, mask):
    hbm = pl.BlockSpec(memory_space=pl.ANY)
    vm = pltpu.VMEM
    dma = pltpu.SemaphoreType.DMA
    unit = jax.ShapeDtypeStruct((1, ROWS, HH), B16)
    own = vm((ROWS, HH), B16)
    outs = pl.pallas_call(
        kernel,
        out_shape=(unit,) * 5 + (jax.ShapeDtypeStruct((OUT_ROWS, D), B16),),
        in_specs=[hbm] * 7 + [pl.BlockSpec(memory_space=pltpu.VMEM)],
        out_specs=(hbm,) * 6,
        scratch_shapes=[
            own, vm((P_SIZE, HH), B16), vm((P_SIZE, HH), B16), vm((HH, D), B16),
            vm((YS * ROWS, D), B16), own, own, own, own, own, vm((YS * ROWS, BLOCK), B16),
            own, own, own, own,
            vm((HEADS, P_SIZE, ROWS), F32), vm((HEADS, ROWS, ROWS), F32),
            vm((P_SIZE, ROWS), F32), vm((ROWS, ROWS), F32),
            vm((BLOCK, YS * ROWS), B16), vm((4, BLOCK, COLS), F32),
            vm((4, BLOCK, COLS), B16), vm((4, BLOCK, COLS), B16),
            vm((4, BLOCK, COLS), B16), vm((16, OUT_ROWS, COLS), B16), vm((OUT_ROWS, COLS), B16),
            vm((ROWS, HH), F32), vm((ROWS, HH), F32), own, own, own, own,
            vm((8, 2 * PIX, HH), B16), vm((GROUPS, ROWS, GC), F32),
            dma((4 + WCH,)), dma((2,)), dma((2,)), dma((6,)), dma((6,)), dma((8,)), dma((7,)),
            dma((GROUPS,)), dma((GROUPS,)), dma, dma((8,)), dma((8, GROUPS)), dma, dma((4,)), dma((4,)), dma,
            dma((8,)), dma, dma, dma((2, GROUPS)), dma((3,)),
        ],
        compiler_params=pltpu.CompilerParams(
            has_side_effects=True, vmem_limit_bytes=62 * 1024 * 1024
        ),
        cost_estimate=pl.CostEstimate(
            flops=8 * 10**9, bytes_accessed=20 * 10**6, transcendentals=3 * 10**6
        ),
    )(qs, ks, vs, qt, kt, up, w, mask)
    return outs[:5] + (outs[5].astype(F32),)


def solution(mesh):
    tokens = P("dp", "seq", None)
    return jax.shard_map(
        local,
        mesh=mesh,
        in_specs=(tokens,) * 6 + (P(), P()),
        out_specs=(tokens,) * 5 + (P("seq", None),),
        check_vma=False,
    )
```

profile of v0, /device:TPU:1, one launch (start us, length us, event | category | flops | bytes accessed | tf_op | source)
XLA Modules:
  0.0 134.0 jit_solution(14243732201955872530)
XLA Ops:
  0.6 126.6 %shard_map.127 = (bf16[1,256,1536]{2,1,0:T(8,128)(2,1)}, bf16[1,256,1536]{2,1,0:T(8,128)(2,1)}, bf16[1,256,1536]{2,1,0:T(8,128)(2,1)}, bf16[1,256,1536]{2,1,0:T(...) custom-call(bf16[1,256,1536]{2,1,0:T(8,128)(2,1)} %qs.1, bf16[1,256,1536]{2,1,0:T(8,128)(2,1)} %ks.1, ...), custom_call_target="tpu_custom_call" | custom-call | flops 8000000000 | bytes 20000000 | tf_op jit(solution)/shard_map/pallas_call | solution.py:406
  127.2 0.0 copy-start.4
  127.3 0.0 copy-start.3
  127.3 2.3 %convert_element_type.3 = f32[96,3072]{1,0:T(8,128)} convert(bf16[96,3072]{1,0:T(8,128)(2,1)} %get-tuple-element.17) | non-fusion elementwise | flops 294912 | bytes 1769472 | tf_op jit(solution)/shard_map/convert_element_type | solution.py:433
  129.6 0.0 copy-done.4
  129.6 0.0 copy-start.2
  129.6 0.9 copy.19
  130.4 0.0 copy-done.3
  130.5 0.0 copy-start.1
  130.5 0.9 copy.20
  131.3 0.0 copy-done.2
  131.3 0.0 copy-start
  131.3 0.9 copy.21
  132.2 0.0 copy-done.1
  132.2 0.9 copy.22
  133.1 0.0 copy-done
  133.1 0.9 copy.23
Async XLA Ops:
  127.2 2.3 %copy-start.4 = (bf16[1,256,1536]{2,1,0:T(8,128)(2,1)S(1)}, bf16[1,256,1536]{2,1,0:T(8,128)(2,1)}, u32[]{:S(2)}) copy-start(bf16[1,256,1536]{2,1,0:T(8,128)(2,1)} %get-tuple-element.24) | copy-start | bytes 2359300
  127.3 3.2 %copy-start.3 = (bf16[1,256,1536]{2,1,0:T(8,128)(2,1)S(1)}, bf16[1,256,1536]{2,1,0:T(8,128)(2,1)}, u32[]{:S(2)}) copy-start(bf16[1,256,1536]{2,1,0:T(8,128)(2,1)} %get-tuple-element.25) | copy-start | bytes 2359300
  129.6 1.8 %copy-start.2 = (bf16[1,256,1536]{2,1,0:T(8,128)(2,1)S(1)}, bf16[1,256,1536]{2,1,0:T(8,128)(2,1)}, u32[]{:S(2)}) copy-start(bf16[1,256,1536]{2,1,0:T(8,128)(2,1)} %get-tuple-element.26) | copy-start | bytes 2359300
  130.5 1.8 %copy-start.1 = (bf16[1,256,1536]{2,1,0:T(8,128)(2,1)S(1)}, bf16[1,256,1536]{2,1,0:T(8,128)(2,1)}, u32[]{:S(2)}) copy-start(bf16[1,256,1536]{2,1,0:T(8,128)(2,1)} %get-tuple-element.27) | copy-start | bytes 2359300
  131.3 1.8 %copy-start = (bf16[1,256,1536]{2,1,0:T(8,128)(2,1)S(1)}, bf16[1,256,1536]{2,1,0:T(8,128)(2,1)}, u32[]{:S(2)}) copy-start(bf16[1,256,1536]{2,1,0:T(8,128)(2,1)} %get-tuple-element.28) | copy-start | bytes 2359300
where the time goes:
time: 134 us
  Pallas kernels  127 us (95%)
  local copies, waits for them, and re-layouts  4.42 us (3%)
  other arithmetic  2.29 us (2%)
    pallas_call x1, Pallas kernels, local(): pl.pallas_call(kernel, out_shape=(unit,) * 5 + (jax.ShapeDtypeStruct((OUT...  127 us
    unnamed x15, local copies, waits for them, and re-layouts  4.42 us

commit v1 on v0

--- a/solution.py
+++ b/solution.py
@@ -43,7 +43,7 @@
     sqg_o, skg_o, svg_o, tqg_o, tkg_o, wg_o,
     q_s, k_s, v_s, w_s, u_s, tq_r, tk_r, so_r, oc_r, sc_r, t_r,
     a_b, b_b, c_b, d_b, pw, tw, bias, tbias, tt, wgf, csend, crecv, rsend, rrecv, red,
-    dk_f, dv_f, dk_x, dv_x, dk_r, dv_r, hop, t_f,
+    dk_f, dv_f, dk_x, dv_x, dk_r, dv_r, hop, t_f, tqg_r, tkg_r, g_r,
     ld, kv_ss, kv_rs, y_ss, y_rs, a2a_ss, a2a_rs, so_rs, sc_rs, t_rs, hop_ss, hop_rs,
     c_ss, c_rs, r_ss, r_rs, g_ss, g_rs, x_ss, x_rs, out_s,
 ):
@@ -115,8 +115,8 @@
     put_oc = putter(oc_r, whole, a2a_rs.at[2])
     put_so = [putter(so_r, group_cols[g], so_rs.at[g]) for g in range(GROUPS)]
     put_sc = [putter(sc_r, group_cols[g], sc_rs.at[g]) for g in range(GROUPS)]
-    put_tqg = putter(tqg_o.at[0], whole, a2a_rs.at[5])
-    put_tkg = putter(tkg_o.at[0], whole, a2a_rs.at[6])
+    put_tqg = putter(tqg_r, whole, a2a_rs.at[5])
+    put_tkg = putter(tkg_r, whole, a2a_rs.at[6])
 
     def put_out(src, src_rows, start, size, ss, xd, zd, zld):
         for k in range(YS):
@@ -130,26 +130,35 @@
     y_up = dev(x, (y + 1) % YS, zh, zl, core)
     y_dn = dev(x, (y + 3) % YS, zh, zl, core)
 
-    send(ks.at[0], k_s.at[pl.ds(ROWS, ROWS)], kv_ss.at[0], kv_rs.at[0], other)
-    send(vs.at[0], v_s.at[pl.ds(ROWS, ROWS)], kv_ss.at[1], kv_rs.at[1], other)
-    local(up.at[0], u_s.at[pl.ds(pl.multiple_of(y * ROWS, ROWS), ROWS)], ld.at[0])
-    for i in range(WCH):
-        local(w.at[pl.ds(i * WROWS, WROWS)], w_s.at[pl.ds(i * WROWS, WROWS)], ld.at[4 + i])
-    local(qs.at[0], q_s, ld.at[1])
-    local(ks.at[0], k_s.at[pl.ds(0, ROWS)], ld.at[2])
-    local(vs.at[0], v_s.at[pl.ds(0, ROWS)], ld.at[3])
     half = ROWS // 2
+    own_k, far_k = pl.ds(0, ROWS), pl.ds(ROWS, ROWS)
+    own_u = pl.ds(pl.multiple_of(y * ROWS, ROWS), ROWS)
 
     def u_half(owner, part):
         return u_s.at[pl.ds(pl.multiple_of(owner * ROWS + part * half, half), half)]
 
-    send(up.at[0, pl.ds(0, half)], u_half(y, 0), y_ss.at[0], y_rs.at[0], y_up)
-    send(up.at[0, pl.ds(half, half)], u_half(y, 1), y_ss.at[1], y_rs.at[1], y_dn)
-
-    spread(qt.at[0], whole, put_tq, 0, 0)
-    spread(kt.at[0], whole, put_tk, 1, 0)
-    send(up.at[0, pl.ds(0, half)], u_half(y, 0), y_ss.at[2], y_rs.at[2], y_dn)
-    send(up.at[0, pl.ds(half, half)], u_half(y, 1), y_ss.at[3], y_rs.at[3], y_up)
+    loads = (
+        (ks.at[0], k_s.at[own_k]), (vs.at[0], v_s.at[own_k]), (qt.at[0], b_b), (kt.at[0], d_b),
+        (up.at[0], u_s.at[own_u]), (qs.at[0], q_s),
+    )
+    for i, (src, dst) in enumerate(loads):
+        local(src, dst, ld.at[i])
+    for i in range(WCH):
+        local(w.at[pl.ds(i * WROWS, WROWS)], w_s.at[pl.ds(i * WROWS, WROWS)], ld.at[6 + i])
+
+    await_bytes(k_s.at[own_k], ld.at[0])
+    send(k_s.at[own_k], k_s.at[far_k], kv_ss.at[0], kv_rs.at[0], other)
+    await_bytes(v_s.at[own_k], ld.at[1])
+    send(v_s.at[own_k], v_s.at[far_k], kv_ss.at[1], kv_rs.at[1], other)
+    await_bytes(b_b, ld.at[2])
+    spread(b_b, whole, put_tq, 0, 0)
+    await_bytes(u_s.at[own_u], ld.at[4])
+    send(u_half(y, 0), u_half(y, 0), y_ss.at[0], y_rs.at[0], y_up)
+    send(u_half(y, 1), u_half(y, 1), y_ss.at[1], y_rs.at[1], y_dn)
+    await_bytes(d_b, ld.at[3])
+    spread(d_b, whole, put_tk, 1, 0)
+    send(u_half(y, 0), u_half(y, 0), y_ss.at[2], y_rs.at[2], y_dn)
+    send(u_half(y, 1), u_half(y, 1), y_ss.at[3], y_rs.at[3], y_up)
 
     key_row = lax.broadcasted_iota(jnp.int32, (P_SIZE, NT), 0)
     key_tile = jnp.where(
@@ -167,52 +176,47 @@
     )
     tbias[...] = jnp.where(same, 0.0, NEG)
 
-    own_u = pl.ds(pl.multiple_of(y * ROWS, ROWS), ROWS)
-    await_bytes(up.at[0], ld.at[0])
-
     for i in range(WCH):
-        await_bytes(w_s.at[pl.ds(i * WROWS, WROWS)], ld.at[4 + i])
+        await_bytes(w_s.at[pl.ds(i * WROWS, WROWS)], ld.at[6 + i])
         c_b[:, pl.ds(i * WROWS, WROWS)] = mm(
             u_s[own_u, :], w_s[pl.ds(i * WROWS, WROWS), :], 1, 1
         ).astype(B16)
 
-    forward(whole, put_tq, 0, 0)
-    forward(whole, put_tk, 1, 0)
-
-    await_bytes(q_s, ld.at[1])
-    await_bytes(k_s.at[pl.ds(0, ROWS)], ld.at[2])
-    await_bytes(v_s.at[pl.ds(0, ROWS)], ld.at[3])
-    await_bytes(k_s.at[pl.ds(ROWS, ROWS)], kv_rs.at[0])
-    await_bytes(v_s.at[pl.ds(ROWS, ROWS)], kv_rs.at[1])
-
-    def space_forward(h, carry):
-        hs = pl.ds(pl.multiple_of(h * HD, HD), HD)
+    await_bytes(q_s, ld.at[5])
+    await_bytes(k_s.at[far_k], kv_rs.at[0])
+    await_bytes(v_s.at[far_k], kv_rs.at[1])
+
+    def space_forward(h):
+        hs = pl.ds(h * HD, HD)
         scores = mm(k_s[:, hs], q_s[:, hs], 1, 1) * SCALE + bias[...]
         powers = jnp.exp(scores - jnp.max(scores, axis=0, keepdims=True))
-        weights = powers / jnp.sum(powers, axis=0, keepdims=True)
+        weights = powers * (1.0 / jnp.sum(powers, axis=0, keepdims=True))
         pw[h] = weights
         a_b[:, hs] = mm(weights.astype(B16), v_s[:, hs], 0, 0).astype(B16)
-        return carry
-
-    for g in range(GROUPS):
-        lax.fori_loop(g * GH, (g + 1) * GH, space_forward, 0)
-
+
+    for g in range(GROUPS):
+        for h in range(g * GH, (g + 1) * GH):
+            space_forward(h)
         spread(a_b, group_cols[g], put_so[g], 3, g)
+        if g == 1:
+            forward(whole, put_tq, 0, 0)
+        if g == 3:
+            forward(whole, put_tk, 1, 0)
 
     spread(c_b, whole, put_oc, 2, 0)
 
     await_bytes(tq_r, a2a_rs.at[0])
     await_bytes(tk_r, a2a_rs.at[1])
 
-    def time_forward(h, carry):
-        hs = pl.ds(pl.multiple_of(h * HD, HD), HD)
+    def time_forward(h):
+        hs = pl.ds(h * HD, HD)
         scores = mm(tk_r[:, hs], tq_r[:, hs], 1, 1) * SCALE + tbias[...]
         powers = jnp.exp(scores - jnp.max(scores, axis=0, keepdims=True))
-        weights = powers / jnp.sum(powers, axis=0, keepdims=True)
+        weights = powers * (1.0 / jnp.sum(powers, axis=0, keepdims=True))
         tw[h] = weights
-        return carry
-
-    lax.fori_loop(0, HEADS, time_forward, 0)
+
+    for h in range(HEADS):
+        time_forward(h)
     for g in range(GROUPS):
         forward(group_cols[g], put_so[g], 3, g)
 
@@ -222,6 +226,7 @@
     await_bytes(u_half(y_p, 1), y_rs.at[1])
     send(u_half(y_p, 1), u_half(y_p, 1), y_ss.at[5], y_rs.at[5], y_dn)
 
+    await_bytes(b_b, a2a_ss.at[0])
     for g in range(GROUPS):
         await_bytes(so_r.at[:, group_cols[g]], so_rs.at[g])
         heads = [
@@ -239,9 +244,10 @@
     await_bytes(oc_r, a2a_rs.at[2])
     await_bytes(c_b, a2a_ss.at[2])
     await_bytes(a_b, a2a_ss.at[3])
-
-    def time_backward(h, carry):
-        hs = pl.ds(pl.multiple_of(h * HD, HD), HD)
+    await_bytes(d_b, a2a_ss.at[1])
+
+    def time_backward(h):
+        hs = pl.ds(h * HD, HD)
         weights = tw[h]
         cot = oc_r[:, hs]
         c_b[:, hs] = mm(weights.astype(B16), cot, 1, 0).astype(B16)
@@ -250,63 +256,24 @@
         grad = (weights * (prob - centre)).astype(B16)
         a_b[:, hs] = (mm(grad, tk_r[:, hs], 0, 0) * SCALE).astype(B16)
         d_b[:, hs] = (mm(grad, tq_r[:, hs], 1, 0) * SCALE).astype(B16)
-        return carry
-
-    for g in range(GROUPS):
-        lax.fori_loop(g * GH, (g + 1) * GH, time_backward, 0)
-
+
+    for g in range(GROUPS):
+        for h in range(g * GH, (g + 1) * GH):
+            time_backward(h)
         spread(c_b, group_cols[g], put_sc[g], 4, g)
         if g == 0:
             forward(whole, put_out, 7, 0)
         else:
             forward(group_cols[g - 1], put_sc[g - 1], 4, g - 1)
 
-    forward(group_cols[GROUPS - 1], put_sc[GROUPS - 1], 4, GROUPS - 1)
-
-    await_bytes(t_r, t_rs)
-    tt[...] = t_r[...].T
-    await_bytes(u_half(y_m, 1), y_rs.at[3])
-    await_bytes(u_half(y_p, 0), y_rs.at[2])
-    y_f = (y + 2) % YS
-    await_bytes(u_half(y_f, 0), y_rs.at[4])
-    await_bytes(u_half(y_f, 1), y_rs.at[5])
-
-    def weight_part(chunk):
-        return mm(tt[...], u_s[:, rows(chunk * COLS, COLS)], 1, 0)
-
-    def pair_sum(i):
-        await_bytes(crecv.at[i], c_rs.at[i])
-        rsend[i] = (wgf[i] + crecv[i].astype(F32)).astype(B16)
-        slot = rrecv.at[x * 4 + zh * 2 + zl]
-        for k in range(4):
-            xd = (x + k) % 4
-            piece = rsend.at[i, rows(xd * OUT_ROWS, OUT_ROWS)]
-            if k > 0:
-                send(piece, slot, r_ss.at[k], r_rs, dev(xd, y, i // 2, i % 2, core))
-            else:
-                mine = zh * 2 + zl == i
-
-                @pl.when(mine)
-                def _():
-                    local(piece, slot, r_rs)
-
-                @pl.when(jnp.logical_not(mine))
-                def _():
-                    send(piece, slot, r_ss.at[0], r_rs, dev(xd, y, i // 2, i % 2, core))
-
-    for i in range(4):
-        csend[i] = weight_part(2 * i + 1 - core).astype(B16)
-        send(csend.at[i], crecv.at[i], c_ss, c_rs.at[i], other)
-        wgf[i] = weight_part(2 * i + core)
-        if i > 0:
-            pair_sum(i - 1)
-    pair_sum(3)
     spread(a_b, whole, put_tqg, 5, 0)
     spread(d_b, whole, put_tkg, 6, 0)
+    forward(group_cols[GROUPS - 1], put_sc[GROUPS - 1], 4, GROUPS - 1)
+
     await_bytes(b_b, a2a_ss.at[7])
 
-    def space_backward(h, carry):
-        hs = pl.ds(pl.multiple_of(h * HD, HD), HD)
+    def space_backward(h):
+        hs = pl.ds(h * HD, HD)
         weights = pw[h]
         cot = sc_r[:, hs]
         key = k_s[:, hs]
@@ -320,20 +287,60 @@
         dv_f[:, hs] = dv[:ROWS]
         dk_x[:, hs] = dk[ROWS:].astype(B16)
         dv_x[:, hs] = dv[ROWS:].astype(B16)
-        return carry
 
     def backward_group(g):
         cols = pl.ds(g * GC, GC)
         await_bytes(sc_r.at[:, cols], sc_rs.at[g])
-        lax.fori_loop(g * GH, (g + 1) * GH, space_backward, 0)
+        for h in range(g * GH, (g + 1) * GH):
+            space_backward(h)
         send(dk_x.at[:, cols], dk_r.at[:, cols], x_ss, x_rs.at[0, g], other)
         send(dv_x.at[:, cols], dv_r.at[:, cols], x_ss, x_rs.at[1, g], other)
 
     for g in range(GROUPS):
         backward_group(g)
-        if g == 0:
+        if g == 1:
             forward(whole, put_tqg, 5, 0)
+        if g == 3:
             forward(whole, put_tkg, 6, 0)
+
+    await_bytes(t_r, t_rs)
+    tt[...] = t_r[...].T
+    await_bytes(u_half(y_m, 1), y_rs.at[3])
+    await_bytes(u_half(y_p, 0), y_rs.at[2])
+    y_f = (y + 2) % YS
+    await_bytes(u_half(y_f, 0), y_rs.at[4])
+    await_bytes(u_half(y_f, 1), y_rs.at[5])
+
+    def weight_part(chunk):
+        return mm(tt[...], u_s[:, rows(chunk * COLS, COLS)], 1, 0)
+
+    def pair_sum(i):
+        await_bytes(crecv.at[i], c_rs.at[i])
+        rsend[i] = (wgf[i] + crecv[i].astype(F32)).astype(B16)
+        slot = rrecv.at[x * 4 + zh * 2 + zl]
+        for k in range(4):
+            xd = (x + k) % 4
+            piece = rsend.at[i, rows(xd * OUT_ROWS, OUT_ROWS)]
+            if k > 0:
+                send(piece, slot, r_ss.at[k], r_rs, dev(xd, y, i // 2, i % 2, core))
+            else:
+                mine = zh * 2 + zl == i
+
+                @pl.when(mine)
+                def _():
+                    local(piece, slot, r_rs)
+
+                @pl.when(jnp.logical_not(mine))
+                def _():
+                    send(piece, slot, r_ss.at[0], r_rs, dev(xd, y, i // 2, i % 2, core))
+
+    for i in range(4):
+        csend[i] = weight_part(2 * i + 1 - core).astype(B16)
+        send(csend.at[i], crecv.at[i], c_ss, c_rs.at[i], other)
+        wgf[i] = weight_part(2 * i + core)
+        if i > 0:
+            pair_sum(i - 1)
+    pair_sum(3)
 
     await_bytes(rrecv, r_rs)
     total = rrecv[0].astype(F32)
@@ -348,11 +355,11 @@
 
         @pl.when(mine)
         def _():
-            local(red, wg_o.at[:, out_cols], g_rs)
+            local(red, g_r.at[:, out_cols], g_rs)
 
         @pl.when(jnp.logical_not(mine))
         def _():
-            send(red, wg_o.at[:, out_cols], g_ss.at[k], g_rs, dev(x, yd, zh_own, zld, core_own))
+            send(red, g_r.at[:, out_cols], g_ss.at[k], g_rs, dev(x, yd, zh_own, zld, core_own))
 
     local(b_b, sqg_o.at[0], out_s.at[0])
     for g in range(GROUPS):
@@ -366,12 +373,15 @@
     dv_x[...] = (dv_f[...] + dv_r[...].astype(F32)).astype(B16)
     local(dv_x, svg_o.at[0], out_s.at[2])
 
-    await_bytes(ks.at[0], kv_ss.at[0])
-    await_bytes(vs.at[0], kv_ss.at[1])
+    await_bytes(tqg_r, a2a_rs.at[5])
+    local(tqg_r, tqg_o.at[0], out_s.at[3])
+    await_bytes(tkg_r, a2a_rs.at[6])
+    local(tkg_r, tkg_o.at[0], out_s.at[4])
+
+    await_bytes(k_s.at[own_k], kv_ss.at[0])
+    await_bytes(v_s.at[own_k], kv_ss.at[1])
     for i in range(6):
         await_bytes(u_half(0, 0), y_ss.at[i])
-    await_bytes(qt.at[0], a2a_ss.at[0])
-    await_bytes(kt.at[0], a2a_ss.at[1])
     await_bytes(c_b, a2a_ss.at[4])
     await_bytes(a_b, a2a_ss.at[5])
     await_bytes(d_b, a2a_ss.at[6])
@@ -389,12 +399,36 @@
         def _():
             await_bytes(red, g_ss.at[k])
 
-    await_bytes(tqg_o.at[0], a2a_rs.at[5])
-    await_bytes(tkg_o.at[0], a2a_rs.at[6])
-    await_bytes(wg_o, g_rs)
+    await_bytes(g_r, g_rs)
+    local(g_r, wg_o, out_s.at[5])
+    await_bytes(tqg_r, out_s.at[3])
+    await_bytes(tkg_r, out_s.at[4])
+    await_bytes(g_r, out_s.at[5])
     await_bytes(b_b, out_s.at[0])
     await_bytes(dk_x, out_s.at[1])
     await_bytes(dv_x, out_s.at[2])
+
+
+def store(a, b, c, d, e, wg, a_o, b_o, c_o, d_o, e_o, wg_o, held, low, wide, loads, stores):
+    ins = [
+        pltpu.make_async_copy(src, dst, loads.at[i])
+        for i, (src, dst) in enumerate(
+            [(wg, low)] + [(r, held.at[pl.ds(k, 1)]) for k, r in enumerate((a, b, c, d, e))]
+        )
+    ]
+    outs = [pltpu.make_async_copy(wide, wg_o, stores.at[0])] + [
+        pltpu.make_async_copy(held.at[pl.ds(k, 1)], r, stores.at[k + 1])
+        for k, r in enumerate((a_o, b_o, c_o, d_o, e_o))
+    ]
+    for copy in ins:
+        copy.start()
+    for k, copy in enumerate(ins):
+        copy.wait()
+        if k == 0:
+            wide[...] = low[...].astype(F32)
+        outs[k].start()
+    for copy in outs:
+        copy.wait()
 
 
 def local(qs, ks, vs, qt, kt, up, w, mask):
@@ -419,9 +453,10 @@
             vm((4, BLOCK, COLS), B16), vm((16, OUT_ROWS, COLS), B16), vm((OUT_ROWS, COLS), B16),
             vm((ROWS, HH), F32), vm((ROWS, HH), F32), own, own, own, own,
             vm((8, 2 * PIX, HH), B16), vm((GROUPS, ROWS, GC), F32),
-            dma((4 + WCH,)), dma((2,)), dma((2,)), dma((6,)), dma((6,)), dma((8,)), dma((7,)),
+            own, own, vm((OUT_ROWS, D), B16),
+            dma((6 + WCH,)), dma((2,)), dma((2,)), dma((6,)), dma((6,)), dma((8,)), dma((7,)),
             dma((GROUPS,)), dma((GROUPS,)), dma, dma((8,)), dma((8, GROUPS)), dma, dma((4,)), dma((4,)), dma,
-            dma((8,)), dma, dma, dma((2, GROUPS)), dma((3,)),
+            dma((8,)), dma, dma, dma((2, GROUPS)), dma((6,)),
         ],
         compiler_params=pltpu.CompilerParams(
             has_side_effects=True, vmem_limit_bytes=62 * 1024 * 1024
@@ -430,7 +465,16 @@
             flops=8 * 10**9, bytes_accessed=20 * 10**6, transcendentals=3 * 10**6
         ),
     )(qs, ks, vs, qt, kt, up, w, mask)
-    return outs[:5] + (outs[5].astype(F32),)
+    return pl.pallas_call(
+        store,
+        out_shape=(unit,) * 5 + (jax.ShapeDtypeStruct((OUT_ROWS, D), F32),),
+        in_specs=[hbm] * 6,
+        out_specs=(hbm,) * 6,
+        scratch_shapes=[
+            vm((5, ROWS, HH), B16), vm((OUT_ROWS, D), B16), vm((OUT_ROWS, D), F32), dma((6,)), dma((6,)),
+        ],
+        compiler_params=pltpu.CompilerParams(vmem_limit_bytes=62 * 1024 * 1024),
+    )(*outs)
 
 
 def solution(mesh):

time: 134 us -> 135 us (level)
  Pallas kernels: 127 us -> 134 us
  local copies, waits for them, and re-layouts: 4.42 us -> 0 us
  other arithmetic: 2.29 us -> 0 us
    unnamed x15 -> x0, local copies, waits for them, and re-layouts: 4.42 us -> none
    pallas_call x1, Pallas kernels: 127 us -> 130 us  [local(): pl.pallas_call(kernel, out_shape=(unit,) * 5 + (jax.ShapeDtypeStruct((OUT...]
    pallas_call x0 -> x1, Pallas kernels: none -> 3.74 us  [local(): pl.pallas_call(store, out_shape=(unit,) * 5 + (jax.ShapeDtypeStruct((OUT_...]
    convert_element_type x1 -> x0, other arithmetic: 2.29 us -> none  [local(): return outs[:5] + (outs[5].astype(F32),)]
where the time goes in v1:
time: 135 us
  Pallas kernels  134 us (99%)
    pallas_call x1, Pallas kernels, local(): pl.pallas_call(kernel, out_shape=(unit,) * 5 + (jax.ShapeDtypeStruct((OUT...  130 us
    pallas_call x1, Pallas kernels, local(): pl.pallas_call(store, out_shape=(unit,) * 5 + (jax.ShapeDtypeStruct((OUT_...  3.74 us

profile of v1, /device:TPU:1, one launch (start us, length us, event | category | flops | bytes accessed | tf_op | source)
XLA Modules:
  0.0 134.9 jit_solution(52427238624200275)
XLA Ops:
  0.6 130.4 %shard_map.127 = (bf16[1,256,1536]{2,1,0:T(8,128)(2,1)}, bf16[1,256,1536]{2,1,0:T(8,128)(2,1)}, bf16[1,256,1536]{2,1,0:T(8,128)(2,1)}, bf16[1,256,1536]{2,1,0:T(...) custom-call(bf16[1,256,1536]{2,1,0:T(8,128)(2,1)} %qs.1, bf16[1,256,1536]{2,1,0:T(8,128)(2,1)} %ks.1, ...), custom_call_target="tpu_custom_call" | custom-call | flops 8000000000 | bytes 20000000 | tf_op jit(solution)/shard_map/pallas_call | solution.py:440
  131.0 3.7 %shard_map.128 = (bf16[1,256,1536]{2,1,0:T(8,128)(2,1)}, bf16[1,256,1536]{2,1,0:T(8,128)(2,1)}, bf16[1,256,1536]{2,1,0:T(8,128)(2,1)}, bf16[1,256,1536]{2,1,0:T(...) custom-call(bf16[1,256,1536]{2,1,0:T(8,128)(2,1)} %get-tuple-element.12.a, ...), custom_call_target="tpu_custom_call" | custom-call | tf_op jit(solution)/shard_map/pallas_call | solution.py:468

commit v2 on v1

--- a/solution.py
+++ b/solution.py
@@ -22,6 +22,8 @@
 BLOCK = HH // YS
 COLS = D // 8
 OUT_ROWS = 96
+SUB = OUT_ROWS // 2
+SIDE = BLOCK // 2
 GROUPS = 4
 GH = HEADS // GROUPS
 GC = GH * HD
@@ -42,7 +44,7 @@
     qs, ks, vs, qt, kt, up, w, mask,
     sqg_o, skg_o, svg_o, tqg_o, tkg_o, wg_o,
     q_s, k_s, v_s, w_s, u_s, tq_r, tk_r, so_r, oc_r, sc_r, t_r,
-    a_b, b_b, c_b, d_b, pw, tw, bias, tbias, tt, wgf, csend, crecv, rsend, rrecv, red,
+    a_b, b_b, c_b, d_b, pw, tw, bias, tbias, tt, wgf, csend, crecv, rsend, ra, rb, ra2, rb2, sa, sb, red,
     dk_f, dv_f, dk_x, dv_x, dk_r, dv_r, hop, t_f, tqg_r, tkg_r, g_r,
     ld, kv_ss, kv_rs, y_ss, y_rs, a2a_ss, a2a_rs, so_rs, sc_rs, t_rs, hop_ss, hop_rs,
     c_ss, c_rs, r_ss, r_rs, g_ss, g_rs, x_ss, x_rs, out_s,
@@ -235,7 +237,11 @@
         ]
         t_f[g] = jnp.concatenate(heads, axis=1)
     for k in range(YS):
-        block = [t_f[g, :, k * OUT_ROWS:(k + 1) * OUT_ROWS] for g in range(GROUPS)]
+        block = [
+            t_f[g, :, k * OUT_ROWS + part * SUB:k * OUT_ROWS + (part + 1) * SUB]
+            for part in range(2)
+            for g in range(GROUPS)
+        ]
         b_b[:, k * BLOCK:(k + 1) * BLOCK] = jnp.concatenate(block, axis=1).astype(B16)
 
     spread(b_b, whole, put_out, 7, 0)
@@ -267,7 +273,6 @@
             forward(group_cols[g - 1], put_sc[g - 1], 4, g - 1)
 
     spread(a_b, whole, put_tqg, 5, 0)
-    spread(d_b, whole, put_tkg, 6, 0)
     forward(group_cols[GROUPS - 1], put_sc[GROUPS - 1], 4, GROUPS - 1)
 
     await_bytes(b_b, a2a_ss.at[7])
@@ -296,12 +301,9 @@
         send(dk_x.at[:, cols], dk_r.at[:, cols], x_ss, x_rs.at[0, g], other)
         send(dv_x.at[:, cols], dv_r.at[:, cols], x_ss, x_rs.at[1, g], other)
 
-    for g in range(GROUPS):
-        backward_group(g)
-        if g == 1:
-            forward(whole, put_tqg, 5, 0)
-        if g == 3:
-            forward(whole, put_tkg, 6, 0)
+    backward_group(0)
+    forward(whole, put_tqg, 5, 0)
+    backward_group(1)
 
     await_bytes(t_r, t_rs)
     tt[...] = t_r[...].T
@@ -311,42 +313,67 @@
     await_bytes(u_half(y_f, 0), y_rs.at[4])
     await_bytes(u_half(y_f, 1), y_rs.at[5])
 
-    def weight_part(chunk):
-        return mm(tt[...], u_s[:, rows(chunk * COLS, COLS)], 1, 0)
-
-    def pair_sum(i):
-        await_bytes(crecv.at[i], c_rs.at[i])
-        rsend[i] = (wgf[i] + crecv[i].astype(F32)).astype(B16)
-        slot = rrecv.at[x * 4 + zh * 2 + zl]
-        for k in range(4):
-            xd = (x + k) % 4
-            piece = rsend.at[i, rows(xd * OUT_ROWS, OUT_ROWS)]
-            if k > 0:
-                send(piece, slot, r_ss.at[k], r_rs, dev(xd, y, i // 2, i % 2, core))
-            else:
-                mine = zh * 2 + zl == i
-
-                @pl.when(mine)
-                def _():
-                    local(piece, slot, r_rs)
-
-                @pl.when(jnp.logical_not(mine))
-                def _():
-                    send(piece, slot, r_ss.at[0], r_rs, dev(xd, y, i // 2, i % 2, core))
-
-    for i in range(4):
-        csend[i] = weight_part(2 * i + 1 - core).astype(B16)
-        send(csend.at[i], crecv.at[i], c_ss, c_rs.at[i], other)
-        wgf[i] = weight_part(2 * i + core)
-        if i > 0:
-            pair_sum(i - 1)
-    pair_sum(3)
-
-    await_bytes(rrecv, r_rs)
-    total = rrecv[0].astype(F32)
-    for k in range(1, 16):
-        total = total + rrecv[k].astype(F32)
-    red[...] = total.astype(B16)
+    z = zh * 2 + zl
+
+    def chip(k):
+        zd = (z + k) % 4
+        return zd // 2, zd % 2
+
+    def weight_part(k, which):
+        zd = (z + k) % 4
+        return mm(tt[...], u_s[:, rows((zd * 2 + which) * COLS, COLS)], 1, 0)
+
+    def pair_sum(k):
+        await_bytes(crecv.at[k], c_rs.at[k])
+        rsend[k] = (wgf[k] + crecv[k].astype(F32)).astype(B16)
+        for step in range(1, 4):
+            xd = (x + step) % 4
+            send(rsend.at[k, rows(xd * SUB, SUB)], ra.at[x, k], r_ss.at[0], r_rs.at[0], dev(xd, y, zh, zl, core))
+        if k > 0:
+            zhd, zld = chip(k)
+            send(rsend.at[k, pl.ds(SIDE, SIDE)], rb.at[z], r_ss.at[1], r_rs.at[1], dev(x, y, zhd, zld, core))
+
+    order = (1, 2, 3, 0)
+    for n, k in enumerate(order):
+        csend[k] = weight_part(k, 1 - core).astype(B16)
+        send(csend.at[k], crecv.at[k], c_ss, c_rs.at[k], other)
+        wgf[k] = weight_part(k, core)
+        if n > 0:
+            pair_sum(order[n - 1])
+    pair_sum(0)
+    spread(d_b, whole, put_tkg, 6, 0)
+    backward_group(2)
+
+    for k in range(4):
+        ra[x, k] = rsend[k, rows(x * SUB, SUB)]
+    rb[z] = rsend[0, SIDE:]
+    await_bytes(ra.at[pl.ds(0, 3)], r_rs.at[0])
+    for k in range(4):
+        total = ra[0, k].astype(F32)
+        for n in range(1, 4):
+            total = total + ra[n, k].astype(F32)
+        sa[k] = total.astype(B16)
+        if k > 0:
+            zhd, zld = chip(k)
+            send(sa.at[k], ra2.at[z], r_ss.at[2], r_rs.at[2], dev(x, y, zhd, zld, core))
+    ra2[z] = sa[0]
+    await_bytes(rb.at[pl.ds(0, 3)], r_rs.at[1])
+    total = rb[0].astype(F32)
+    for n in range(1, 4):
+        total = total + rb[n].astype(F32)
+    sb[...] = total.astype(B16)
+    for step in range(1, 4):
+        xd = (x + step) % 4
+        send(sb.at[rows(xd * SUB, SUB)], rb2.at[x], r_ss.at[3], r_rs.at[3], dev(xd, y, zh, zl, core))
+    rb2[x] = sb[rows(x * SUB, SUB)]
+    backward_group(3)
+
+    for part, (held, n) in enumerate(((ra2, 2), (rb2, 3))):
+        await_bytes(held.at[pl.ds(0, 3)], r_rs.at[n])
+        total = held[0].astype(F32)
+        for k in range(1, 4):
+            total = total + held[k].astype(F32)
+        red[part * SUB:(part + 1) * SUB] = total.astype(B16)
     out_cols = rows(((zh * 2 + zl) * 2 + core) * COLS, COLS)
     zh_own, core_own = y // 2, y % 2
     for k in range(8):
@@ -360,6 +387,8 @@
         @pl.when(jnp.logical_not(mine))
         def _():
             send(red, g_r.at[:, out_cols], g_ss.at[k], g_rs, dev(x, yd, zh_own, zld, core_own))
+
+    forward(whole, put_tkg, 6, 0)
 
     local(b_b, sqg_o.at[0], out_s.at[0])
     for g in range(GROUPS):
@@ -388,9 +417,8 @@
     for unit in range(8):
         await_bytes(hop.at[unit], hop_ss.at[unit])
     await_bytes(csend, c_ss)
-    for k in range(1, 4):
-        await_bytes(rsend.at[0], r_ss.at[k])
-    await_bytes(rsend.at[0, pl.ds(0, 3 * OUT_ROWS)], r_ss.at[0])
+    for n, held in enumerate((ra, rb, ra2, rb2)):
+        await_bytes(held.at[pl.ds(0, 3)], r_ss.at[n])
     for k in range(8):
         yd, zld = (y + k // 2) % YS, (zl + k) % 2
         mine = (yd == y) & (zh_own == zh) & (zld == zl) & (core_own == core)
@@ -450,12 +478,14 @@
             vm((P_SIZE, ROWS), F32), vm((ROWS, ROWS), F32),
             vm((BLOCK, YS * ROWS), B16), vm((4, BLOCK, COLS), F32),
             vm((4, BLOCK, COLS), B16), vm((4, BLOCK, COLS), B16),
-            vm((4, BLOCK, COLS), B16), vm((16, OUT_ROWS, COLS), B16), vm((OUT_ROWS, COLS), B16),
+            vm((4, BLOCK, COLS), B16), vm((4, 4, SUB, COLS), B16), vm((4, SIDE, COLS), B16),
+            vm((4, SUB, COLS), B16), vm((4, SUB, COLS), B16), vm((4, SUB, COLS), B16),
+            vm((SIDE, COLS), B16), vm((OUT_ROWS, COLS), B16),
             vm((ROWS, HH), F32), vm((ROWS, HH), F32), own, own, own, own,
             vm((8, 2 * PIX, HH), B16), vm((GROUPS, ROWS, GC), F32),
             own, own, vm((OUT_ROWS, D), B16),
             dma((6 + WCH,)), dma((2,)), dma((2,)), dma((6,)), dma((6,)), dma((8,)), dma((7,)),
-            dma((GROUPS,)), dma((GROUPS,)), dma, dma((8,)), dma((8, GROUPS)), dma, dma((4,)), dma((4,)), dma,
+            dma((GROUPS,)), dma((GROUPS,)), dma, dma((8,)), dma((8, GROUPS)), dma, dma((4,)), dma((4,)), dma((4,)),
             dma((8,)), dma, dma, dma((2, GROUPS)), dma((6,)),
         ],
         compiler_params=pltpu.CompilerParams(

time: 135 us -> 122 us (0.904)
  Pallas kernels: 134 us -> 121 us
    pallas_call x1, Pallas kernels: 130 us -> 118 us  [local(): pl.pallas_call(kernel, out_shape=(unit,) * 5 + (jax.ShapeDtypeStruct((OUT...]
where the time goes in v2:
time: 122 us
  Pallas kernels  121 us (99%)
    pallas_call x1, Pallas kernels, local(): pl.pallas_call(kernel, out_shape=(unit,) * 5 + (jax.ShapeDtypeStruct((OUT...  118 us
    pallas_call x1, Pallas kernels, local(): pl.pallas_call(store, out_shape=(unit,) * 5 + (jax.ShapeDtypeStruct((OUT_...  3.74 us

profile of v2, /device:TPU:1, one launch (start us, length us, event | category | flops | bytes accessed | tf_op | source)
XLA Modules:
  0.0 122.2 jit_solution(17775886340276316085)
XLA Ops:
  0.6 117.6 %shard_map.127 = (bf16[1,256,1536]{2,1,0:T(8,128)(2,1)}, bf16[1,256,1536]{2,1,0:T(8,128)(2,1)}, bf16[1,256,1536]{2,1,0:T(8,128)(2,1)}, bf16[1,256,1536]{2,1,0:T(...) custom-call(bf16[1,256,1536]{2,1,0:T(8,128)(2,1)} %qs.1, bf16[1,256,1536]{2,1,0:T(8,128)(2,1)} %ks.1, ...), custom_call_target="tpu_custom_call" | custom-call | flops 8000000000 | bytes 20000000 | tf_op jit(solution)/shard_map/pallas_call | solution.py:468
  118.3 3.7 %shard_map.128 = (bf16[1,256,1536]{2,1,0:T(8,128)(2,1)}, bf16[1,256,1536]{2,1,0:T(8,128)(2,1)}, bf16[1,256,1536]{2,1,0:T(8,128)(2,1)}, bf16[1,256,1536]{2,1,0:T(...) custom-call(bf16[1,256,1536]{2,1,0:T(8,128)(2,1)} %get-tuple-element.12.a, ...), custom_call_target="tpu_custom_call" | custom-call | tf_op jit(solution)/shard_map/pallas_call | solution.py:498

commit v3 on v2

--- a/solution.py
+++ b/solution.py
@@ -30,7 +30,10 @@
 WCH = 6
 WROWS = HH // WCH
 SCALE = 1.0 / math.sqrt(HD)
+POWER = SCALE / math.log(2.0)
 NEG = -1e30
+BAND = PIX // 2
+GROUP = ROWS // 2
 MESH = pl.DeviceIdType.MESH
 F32 = jnp.float32
 B16 = jnp.bfloat16
@@ -173,16 +176,16 @@
     rows_mask = mm(query_hot, mask[...].astype(F32), 1, 0)
     bias[...] = jnp.where(mm(key_hot, rows_mask, 1, 1) > 0.5, 0.0, NEG)
     same = (
-        lax.broadcasted_iota(jnp.int32, (ROWS, ROWS), 0) % PIX
-        == lax.broadcasted_iota(jnp.int32, (ROWS, ROWS), 1) % PIX
+        lax.broadcasted_iota(jnp.int32, (GROUP, GROUP), 0) % BAND
+        == lax.broadcasted_iota(jnp.int32, (GROUP, GROUP), 1) % BAND
     )
     tbias[...] = jnp.where(same, 0.0, NEG)
 
     for i in range(WCH):
         await_bytes(w_s.at[pl.ds(i * WROWS, WROWS)], ld.at[6 + i])
         c_b[:, pl.ds(i * WROWS, WROWS)] = mm(
-            u_s[own_u, :], w_s[pl.ds(i * WROWS, WROWS), :], 1, 1
-        ).astype(B16)
+            w_s[pl.ds(i * WROWS, WROWS), :], u_s[own_u, :], 1, 1
+        ).T.astype(B16)
 
     await_bytes(q_s, ld.at[5])
     await_bytes(k_s.at[far_k], kv_rs.at[0])
@@ -190,8 +193,8 @@
 
     def space_forward(h):
         hs = pl.ds(h * HD, HD)
-        scores = mm(k_s[:, hs], q_s[:, hs], 1, 1) * SCALE + bias[...]
-        powers = jnp.exp(scores - jnp.max(scores, axis=0, keepdims=True))
+        scores = mm(k_s[:, hs], q_s[:, hs], 1, 1) + bias[...]
+        powers = jnp.exp2((scores - jnp.max(scores, axis=0, keepdims=True)) * POWER)
         weights = powers * (1.0 / jnp.sum(powers, axis=0, keepdims=True))
         pw[h] = weights
         a_b[:, hs] = mm(weights.astype(B16), v_s[:, hs], 0, 0).astype(B16)
@@ -210,12 +213,22 @@
     await_bytes(tq_r, a2a_rs.at[0])
     await_bytes(tk_r, a2a_rs.at[1])
 
+    def band(ref, h, b):
+        hs = pl.ds(h * HD, HD)
+        return jnp.concatenate(
+            [ref[f * PIX + b * BAND:f * PIX + (b + 1) * BAND, hs] for f in range(FRAMES)], axis=0
+        )
+
+    def put_band(ref, h, b, value):
+        hs = pl.ds(h * HD, HD)
+        for f in range(FRAMES):
+            ref[f * PIX + b * BAND:f * PIX + (b + 1) * BAND, hs] = value[f * BAND:(f + 1) * BAND]
+
     def time_forward(h):
-        hs = pl.ds(h * HD, HD)
-        scores = mm(tk_r[:, hs], tq_r[:, hs], 1, 1) * SCALE + tbias[...]
-        powers = jnp.exp(scores - jnp.max(scores, axis=0, keepdims=True))
-        weights = powers * (1.0 / jnp.sum(powers, axis=0, keepdims=True))
-        tw[h] = weights
+        for b in range(2):
+            scores = mm(band(tk_r, h, b), band(tq_r, h, b), 1, 1) + tbias[...]
+            powers = jnp.exp2((scores - jnp.max(scores, axis=0, keepdims=True)) * POWER)
+            tw[h, b] = powers * (1.0 / jnp.sum(powers, axis=0, keepdims=True))
 
     for h in range(HEADS):
         time_forward(h)
@@ -231,11 +244,14 @@
     await_bytes(b_b, a2a_ss.at[0])
     for g in range(GROUPS):
         await_bytes(so_r.at[:, group_cols[g]], so_rs.at[g])
-        heads = [
-            mm(tw[h].astype(B16), so_r[:, h * HD:(h + 1) * HD], 0, 0)
-            for h in range(g * GH, (g + 1) * GH)
-        ]
-        t_f[g] = jnp.concatenate(heads, axis=1)
+        for n in range(GH):
+            h = g * GH + n
+            for b in range(2):
+                out = mm(tw[h, b].astype(B16), band(so_r, h, b), 0, 0)
+                for f in range(FRAMES):
+                    t_f[g, f * PIX + b * BAND:f * PIX + (b + 1) * BAND, n * HD:(n + 1) * HD] = (
+                        out[f * BAND:(f + 1) * BAND]
+                    )
     for k in range(YS):
         block = [
             t_f[g, :, k * OUT_ROWS + part * SUB:k * OUT_ROWS + (part + 1) * SUB]
@@ -253,15 +269,15 @@
     await_bytes(d_b, a2a_ss.at[1])
 
     def time_backward(h):
-        hs = pl.ds(h * HD, HD)
-        weights = tw[h]
-        cot = oc_r[:, hs]
-        c_b[:, hs] = mm(weights.astype(B16), cot, 1, 0).astype(B16)
-        prob = mm(so_r[:, hs], cot, 1, 1)
-        centre = jnp.sum(weights * prob, axis=0, keepdims=True)
-        grad = (weights * (prob - centre)).astype(B16)
-        a_b[:, hs] = (mm(grad, tk_r[:, hs], 0, 0) * SCALE).astype(B16)
-        d_b[:, hs] = (mm(grad, tq_r[:, hs], 1, 0) * SCALE).astype(B16)
+        for b in range(2):
+            weights = tw[h, b]
+            cot = band(oc_r, h, b)
+            put_band(c_b, h, b, mm(weights.astype(B16), cot, 1, 0).astype(B16))
+            prob = mm(band(so_r, h, b), cot, 1, 1)
+            centre = jnp.sum(weights * prob, axis=0, keepdims=True)
+            grad = (weights * (prob - centre)).astype(B16)
+            put_band(a_b, h, b, (mm(grad, band(tk_r, h, b), 0, 0) * SCALE).astype(B16))
+            put_band(d_b, h, b, (mm(grad, band(tq_r, h, b), 1, 0) * SCALE).astype(B16))
 
     for g in range(GROUPS):
         for h in range(g * GH, (g + 1) * GH):
@@ -273,7 +289,6 @@
             forward(group_cols[g - 1], put_sc[g - 1], 4, g - 1)
 
     spread(a_b, whole, put_tqg, 5, 0)
-    forward(group_cols[GROUPS - 1], put_sc[GROUPS - 1], 4, GROUPS - 1)
 
     await_bytes(b_b, a2a_ss.at[7])
 
@@ -301,12 +316,9 @@
         send(dk_x.at[:, cols], dk_r.at[:, cols], x_ss, x_rs.at[0, g], other)
         send(dv_x.at[:, cols], dv_r.at[:, cols], x_ss, x_rs.at[1, g], other)
 
-    backward_group(0)
-    forward(whole, put_tqg, 5, 0)
-    backward_group(1)
-
     await_bytes(t_r, t_rs)
     tt[...] = t_r[...].T
+    forward(group_cols[GROUPS - 1], put_sc[GROUPS - 1], 4, GROUPS - 1)
     await_bytes(u_half(y_m, 1), y_rs.at[3])
     await_bytes(u_half(y_p, 0), y_rs.at[2])
     y_f = (y + 2) % YS
@@ -319,13 +331,15 @@
         zd = (z + k) % 4
         return zd // 2, zd % 2
 
-    def weight_part(k, which):
+    def weight_part(k):
         zd = (z + k) % 4
-        return mm(tt[...], u_s[:, rows((zd * 2 + which) * COLS, COLS)], 1, 0)
+        part = mm(tt[...], u_s[:, rows(zd * 2 * COLS, 2 * COLS)], 1, 0)
+        wgf[k, 0] = part[:, :COLS]
+        wgf[k, 1] = part[:, COLS:]
 
     def pair_sum(k):
         await_bytes(crecv.at[k], c_rs.at[k])
-        rsend[k] = (wgf[k] + crecv[k].astype(F32)).astype(B16)
+        rsend[k] = (wgf[k, core] + crecv[k].astype(F32)).astype(B16)
         for step in range(1, 4):
             xd = (x + step) % 4
             send(rsend.at[k, rows(xd * SUB, SUB)], ra.at[x, k], r_ss.at[0], r_rs.at[0], dev(xd, y, zh, zl, core))
@@ -335,14 +349,15 @@
 
     order = (1, 2, 3, 0)
     for n, k in enumerate(order):
-        csend[k] = weight_part(k, 1 - core).astype(B16)
+        weight_part(k)
+        csend[k] = wgf[k, 1 - core].astype(B16)
         send(csend.at[k], crecv.at[k], c_ss, c_rs.at[k], other)
-        wgf[k] = weight_part(k, core)
         if n > 0:
             pair_sum(order[n - 1])
     pair_sum(0)
     spread(d_b, whole, put_tkg, 6, 0)
-    backward_group(2)
+    forward(whole, put_tqg, 5, 0)
+    backward_group(0)
 
     for k in range(4):
         ra[x, k] = rsend[k, rows(x * SUB, SUB)]
@@ -366,7 +381,7 @@
         xd = (x + step) % 4
         send(sb.at[rows(xd * SUB, SUB)], rb2.at[x], r_ss.at[3], r_rs.at[3], dev(xd, y, zh, zl, core))
     rb2[x] = sb[rows(x * SUB, SUB)]
-    backward_group(3)
+    backward_group(1)
 
     for part, (held, n) in enumerate(((ra2, 2), (rb2, 3))):
         await_bytes(held.at[pl.ds(0, 3)], r_rs.at[n])
@@ -389,6 +404,8 @@
             send(red, g_r.at[:, out_cols], g_ss.at[k], g_rs, dev(x, yd, zh_own, zld, core_own))
 
     forward(whole, put_tkg, 6, 0)
+    backward_group(2)
+    backward_group(3)
 
     local(b_b, sqg_o.at[0], out_s.at[0])
     for g in range(GROUPS):
@@ -474,9 +491,9 @@
             own, vm((P_SIZE, HH), B16), vm((P_SIZE, HH), B16), vm((HH, D), B16),
             vm((YS * ROWS, D), B16), own, own, own, own, own, vm((YS * ROWS, BLOCK), B16),
             own, own, own, own,
-            vm((HEADS, P_SIZE, ROWS), F32), vm((HEADS, ROWS, ROWS), F32),
-            vm((P_SIZE, ROWS), F32), vm((ROWS, ROWS), F32),
-            vm((BLOCK, YS * ROWS), B16), vm((4, BLOCK, COLS), F32),
+            vm((HEADS, P_SIZE, ROWS), F32), vm((HEADS, 2, GROUP, GROUP), F32),
+            vm((P_SIZE, ROWS), F32), vm((GROUP, GROUP), F32),
+            vm((BLOCK, YS * ROWS), B16), vm((4, 2, BLOCK, COLS), F32),
             vm((4, BLOCK, COLS), B16), vm((4, BLOCK, COLS), B16),
             vm((4, BLOCK, COLS), B16), vm((4, 4, SUB, COLS), B16), vm((4, SIDE, COLS), B16),
             vm((4, SUB, COLS), B16), vm((4, SUB, COLS), B16), vm((4, SUB, COLS), B16),

time: 122 us -> 121 us (level)
  no operation moved by 1% of the time
where the time goes in v3:
time: 121 us
  Pallas kernels  120 us (99%)
    pallas_call x1, Pallas kernels, local(): pl.pallas_call(kernel, out_shape=(unit,) * 5 + (jax.ShapeDtypeStruct((OUT...  117 us
    pallas_call x1, Pallas kernels, local(): pl.pallas_call(store, out_shape=(unit,) * 5 + (jax.ShapeDtypeStruct((OUT_...  3.74 us

profile of v3, /device:TPU:1, one launch (start us, length us, event | category | flops | bytes accessed | tf_op | source)
XLA Modules:
  0.0 121.3 jit_solution(1774440858286464692)
XLA Ops:
  0.6 116.7 %shard_map.127 = (bf16[1,256,1536]{2,1,0:T(8,128)(2,1)}, bf16[1,256,1536]{2,1,0:T(8,128)(2,1)}, bf16[1,256,1536]{2,1,0:T(8,128)(2,1)}, bf16[1,256,1536]{2,1,0:T(...) custom-call(bf16[1,256,1536]{2,1,0:T(8,128)(2,1)} %qs.1, bf16[1,256,1536]{2,1,0:T(8,128)(2,1)} %ks.1, ...), custom_call_target="tpu_custom_call" | custom-call | flops 8000000000 | bytes 20000000 | tf_op jit(solution)/shard_map/pallas_call | solution.py:485
  117.4 3.7 %shard_map.128 = (bf16[1,256,1536]{2,1,0:T(8,128)(2,1)}, bf16[1,256,1536]{2,1,0:T(8,128)(2,1)}, bf16[1,256,1536]{2,1,0:T(8,128)(2,1)}, bf16[1,256,1536]{2,1,0:T(...) custom-call(bf16[1,256,1536]{2,1,0:T(8,128)(2,1)} %get-tuple-element.12.a, ...), custom_call_target="tpu_custom_call" | custom-call | tf_op jit(solution)/shard_map/pallas_call | solution.py:515

commit v4 on v3

--- a/solution.py
+++ b/solution.py
@@ -135,12 +135,13 @@
     y_up = dev(x, (y + 1) % YS, zh, zl, core)
     y_dn = dev(x, (y + 3) % YS, zh, zl, core)
 
-    half = ROWS // 2
+    cut = 160
     own_k, far_k = pl.ds(0, ROWS), pl.ds(ROWS, ROWS)
     own_u = pl.ds(pl.multiple_of(y * ROWS, ROWS), ROWS)
 
     def u_half(owner, part):
-        return u_s.at[pl.ds(pl.multiple_of(owner * ROWS + part * half, half), half)]
+        start, size = (0, cut) if part == 0 else (cut, ROWS - cut)
+        return u_s.at[pl.ds(pl.multiple_of(owner * ROWS + start, PIX), size)]
 
     loads = (
         (ks.at[0], k_s.at[own_k]), (vs.at[0], v_s.at[own_k]), (qt.at[0], b_b), (kt.at[0], d_b),
@@ -210,6 +211,12 @@
 
     spread(c_b, whole, put_oc, 2, 0)
 
+    y_m, y_p = (y + 3) % YS, (y + 1) % YS
+    await_bytes(u_half(y_m, 0), y_rs.at[0])
+    send(u_half(y_m, 0), u_half(y_m, 0), y_ss.at[4], y_rs.at[4], y_up)
+    await_bytes(u_half(y_p, 1), y_rs.at[1])
+    send(u_half(y_p, 1), u_half(y_p, 1), y_ss.at[5], y_rs.at[5], y_dn)
+
     await_bytes(tq_r, a2a_rs.at[0])
     await_bytes(tk_r, a2a_rs.at[1])
 
@@ -234,12 +241,6 @@
         time_forward(h)
     for g in range(GROUPS):
         forward(group_cols[g], put_so[g], 3, g)
-
-    y_m, y_p = (y + 3) % YS, (y + 1) % YS
-    await_bytes(u_half(y_m, 0), y_rs.at[0])
-    send(u_half(y_m, 0), u_half(y_m, 0), y_ss.at[4], y_rs.at[4], y_up)
-    await_bytes(u_half(y_p, 1), y_rs.at[1])
-    send(u_half(y_p, 1), u_half(y_p, 1), y_ss.at[5], y_rs.at[5], y_dn)
 
     await_bytes(b_b, a2a_ss.at[0])
     for g in range(GROUPS):
@@ -289,6 +290,8 @@
             forward(group_cols[g - 1], put_sc[g - 1], 4, g - 1)
 
     spread(a_b, whole, put_tqg, 5, 0)
+    forward(group_cols[GROUPS - 1], put_sc[GROUPS - 1], 4, GROUPS - 1)
+    spread(d_b, whole, put_tkg, 6, 0)
 
     await_bytes(b_b, a2a_ss.at[7])
 
@@ -316,9 +319,13 @@
         send(dk_x.at[:, cols], dk_r.at[:, cols], x_ss, x_rs.at[0, g], other)
         send(dv_x.at[:, cols], dv_r.at[:, cols], x_ss, x_rs.at[1, g], other)
 
+    backward_group(0)
+    forward(whole, put_tqg, 5, 0)
+    backward_group(1)
+    forward(whole, put_tkg, 6, 0)
+
     await_bytes(t_r, t_rs)
     tt[...] = t_r[...].T
-    forward(group_cols[GROUPS - 1], put_sc[GROUPS - 1], 4, GROUPS - 1)
     await_bytes(u_half(y_m, 1), y_rs.at[3])
     await_bytes(u_half(y_p, 0), y_rs.at[2])
     y_f = (y + 2) % YS
@@ -355,9 +362,7 @@
         if n > 0:
             pair_sum(order[n - 1])
     pair_sum(0)
-    spread(d_b, whole, put_tkg, 6, 0)
-    forward(whole, put_tqg, 5, 0)
-    backward_group(0)
+    backward_group(2)
 
     for k in range(4):
         ra[x, k] = rsend[k, rows(x * SUB, SUB)]
@@ -381,7 +386,7 @@
         xd = (x + step) % 4
         send(sb.at[rows(xd * SUB, SUB)], rb2.at[x], r_ss.at[3], r_rs.at[3], dev(xd, y, zh, zl, core))
     rb2[x] = sb[rows(x * SUB, SUB)]
-    backward_group(1)
+    backward_group(3)
 
     for part, (held, n) in enumerate(((ra2, 2), (rb2, 3))):
         await_bytes(held.at[pl.ds(0, 3)], r_rs.at[n])
@@ -403,10 +408,6 @@
         def _():
             send(red, g_r.at[:, out_cols], g_ss.at[k], g_rs, dev(x, yd, zh_own, zld, core_own))
 
-    forward(whole, put_tkg, 6, 0)
-    backward_group(2)
-    backward_group(3)
-
     local(b_b, sqg_o.at[0], out_s.at[0])
     for g in range(GROUPS):
         cols = pl.ds(g * GC, GC)
@@ -426,8 +427,8 @@
 
     await_bytes(k_s.at[own_k], kv_ss.at[0])
     await_bytes(v_s.at[own_k], kv_ss.at[1])
-    for i in range(6):
-        await_bytes(u_half(0, 0), y_ss.at[i])
+    for i, part in enumerate((0, 1, 0, 1, 0, 1)):
+        await_bytes(u_half(0, part), y_ss.at[i])
     await_bytes(c_b, a2a_ss.at[4])
     await_bytes(a_b, a2a_ss.at[5])
     await_bytes(d_b, a2a_ss.at[6])

time: 121 us -> 124 us (1.025)
  Pallas kernels: 120 us -> 123 us
    pallas_call x1, Pallas kernels: 117 us -> 119 us  [local(): pl.pallas_call(kernel, out_shape=(unit,) * 5 + (jax.ShapeDtypeStruct((OUT...]
where the time goes in v4:
time: 124 us
  Pallas kernels  123 us (99%)
    pallas_call x1, Pallas kernels, local(): pl.pallas_call(kernel, out_shape=(unit,) * 5 + (jax.ShapeDtypeStruct((OUT...  119 us
    pallas_call x1, Pallas kernels, local(): pl.pallas_call(store, out_shape=(unit,) * 5 + (jax.ShapeDtypeStruct((OUT_...  3.74 us

profile of v4, /device:TPU:1, one launch (start us, length us, event | category | flops | bytes accessed | tf_op | source)
XLA Modules:
  0.0 123.8 jit_solution(18077925680515217754)
XLA Ops:
  0.6 119.3 %shard_map.127 = (bf16[1,256,1536]{2,1,0:T(8,128)(2,1)}, bf16[1,256,1536]{2,1,0:T(8,128)(2,1)}, bf16[1,256,1536]{2,1,0:T(8,128)(2,1)}, bf16[1,256,1536]{2,1,0:T(...) custom-call(bf16[1,256,1536]{2,1,0:T(8,128)(2,1)} %qs.1, bf16[1,256,1536]{2,1,0:T(8,128)(2,1)} %ks.1, ...), custom_call_target="tpu_custom_call" | custom-call | flops 8000000000 | bytes 20000000 | tf_op jit(solution)/shard_map/pallas_call | solution.py:486
  119.9 3.7 %shard_map.128 = (bf16[1,256,1536]{2,1,0:T(8,128)(2,1)}, bf16[1,256,1536]{2,1,0:T(8,128)(2,1)}, bf16[1,256,1536]{2,1,0:T(8,128)(2,1)}, bf16[1,256,1536]{2,1,0:T(...) custom-call(bf16[1,256,1536]{2,1,0:T(8,128)(2,1)} %get-tuple-element.12.a, ...), custom_call_target="tpu_custom_call" | custom-call | tf_op jit(solution)/shard_map/pallas_call | solution.py:516

commit v5 on v3

--- a/solution.py
+++ b/solution.py
@@ -114,12 +114,20 @@
         return put
 
     whole = pl.ds(0, HH)
-    group_cols = [pl.ds(g * GC, GC) for g in range(GROUPS)]
+
+    def group_cols(g):
+        return rows(g * GC, GC)
+
     put_tq = putter(tq_r, whole, a2a_rs.at[0])
     put_tk = putter(tk_r, whole, a2a_rs.at[1])
     put_oc = putter(oc_r, whole, a2a_rs.at[2])
-    put_so = [putter(so_r, group_cols[g], so_rs.at[g]) for g in range(GROUPS)]
-    put_sc = [putter(sc_r, group_cols[g], sc_rs.at[g]) for g in range(GROUPS)]
+
+    def put_so(g):
+        return putter(so_r, group_cols(g), so_rs.at[g])
+
+    def put_sc(g):
+        return putter(sc_r, group_cols(g), sc_rs.at[g])
+
     put_tqg = putter(tqg_r, whole, a2a_rs.at[5])
     put_tkg = putter(tkg_r, whole, a2a_rs.at[6])
 
@@ -181,46 +189,48 @@
     )
     tbias[...] = jnp.where(same, 0.0, NEG)
 
-    for i in range(WCH):
-        await_bytes(w_s.at[pl.ds(i * WROWS, WROWS)], ld.at[6 + i])
-        c_b[:, pl.ds(i * WROWS, WROWS)] = mm(
-            w_s[pl.ds(i * WROWS, WROWS), :], u_s[own_u, :], 1, 1
-        ).T.astype(B16)
+    def cot_chunk(i, carry):
+        part = rows(i * WROWS, WROWS)
+        await_bytes(w_s.at[part], ld.at[6 + i])
+        c_b[:, part] = mm(w_s[part, :], u_s[own_u, :], 1, 1).T.astype(B16)
+        return carry
+
+    lax.fori_loop(0, WCH, cot_chunk, 0)
 
     await_bytes(q_s, ld.at[5])
     await_bytes(k_s.at[far_k], kv_rs.at[0])
     await_bytes(v_s.at[far_k], kv_rs.at[1])
 
     def space_forward(h):
-        hs = pl.ds(h * HD, HD)
+        hs = rows(h * HD, HD)
         scores = mm(k_s[:, hs], q_s[:, hs], 1, 1) + bias[...]
         powers = jnp.exp2((scores - jnp.max(scores, axis=0, keepdims=True)) * POWER)
         weights = powers * (1.0 / jnp.sum(powers, axis=0, keepdims=True))
         pw[h] = weights
         a_b[:, hs] = mm(weights.astype(B16), v_s[:, hs], 0, 0).astype(B16)
 
-    for g in range(GROUPS):
-        for h in range(g * GH, (g + 1) * GH):
-            space_forward(h)
-        spread(a_b, group_cols[g], put_so[g], 3, g)
-        if g == 1:
-            forward(whole, put_tq, 0, 0)
-        if g == 3:
-            forward(whole, put_tk, 1, 0)
-
+    def space_group(g, carry):
+        for n in range(GH):
+            space_forward(g * GH + n)
+        spread(a_b, group_cols(g), put_so(g), 3, g)
+        return carry
+
+    lax.fori_loop(0, GROUPS, space_group, 0)
+    forward(whole, put_tq, 0, 0)
+    forward(whole, put_tk, 1, 0)
     spread(c_b, whole, put_oc, 2, 0)
 
     await_bytes(tq_r, a2a_rs.at[0])
     await_bytes(tk_r, a2a_rs.at[1])
 
     def band(ref, h, b):
-        hs = pl.ds(h * HD, HD)
+        hs = rows(h * HD, HD)
         return jnp.concatenate(
             [ref[f * PIX + b * BAND:f * PIX + (b + 1) * BAND, hs] for f in range(FRAMES)], axis=0
         )
 
     def put_band(ref, h, b, value):
-        hs = pl.ds(h * HD, HD)
+        hs = rows(h * HD, HD)
         for f in range(FRAMES):
             ref[f * PIX + b * BAND:f * PIX + (b + 1) * BAND, hs] = value[f * BAND:(f + 1) * BAND]
 
@@ -230,10 +240,18 @@
             powers = jnp.exp2((scores - jnp.max(scores, axis=0, keepdims=True)) * POWER)
             tw[h, b] = powers * (1.0 / jnp.sum(powers, axis=0, keepdims=True))
 
-    for h in range(HEADS):
-        time_forward(h)
-    for g in range(GROUPS):
-        forward(group_cols[g], put_so[g], 3, g)
+    def time_group(g, carry):
+        for n in range(GH):
+            time_forward(g * GH + n)
+        return carry
+
+    lax.fori_loop(0, GROUPS, time_group, 0)
+
+    def forward_space(g, carry):
+        forward(group_cols(g), put_so(g), 3, g)
+        return carry
+
+    lax.fori_loop(0, GROUPS, forward_space, 0)
 
     y_m, y_p = (y + 3) % YS, (y + 1) % YS
     await_bytes(u_half(y_m, 0), y_rs.at[0])
@@ -242,8 +260,8 @@
     send(u_half(y_p, 1), u_half(y_p, 1), y_ss.at[5], y_rs.at[5], y_dn)
 
     await_bytes(b_b, a2a_ss.at[0])
-    for g in range(GROUPS):
-        await_bytes(so_r.at[:, group_cols[g]], so_rs.at[g])
+    def apply_group(g, carry):
+        await_bytes(so_r.at[:, group_cols(g)], so_rs.at[g])
         for n in range(GH):
             h = g * GH + n
             for b in range(2):
@@ -252,6 +270,9 @@
                     t_f[g, f * PIX + b * BAND:f * PIX + (b + 1) * BAND, n * HD:(n + 1) * HD] = (
                         out[f * BAND:(f + 1) * BAND]
                     )
+        return carry
+
+    lax.fori_loop(0, GROUPS, apply_group, 0)
     for k in range(YS):
         block = [
             t_f[g, :, k * OUT_ROWS + part * SUB:k * OUT_ROWS + (part + 1) * SUB]
@@ -279,21 +300,28 @@
             put_band(a_b, h, b, (mm(grad, band(tk_r, h, b), 0, 0) * SCALE).astype(B16))
             put_band(d_b, h, b, (mm(grad, band(tq_r, h, b), 1, 0) * SCALE).astype(B16))
 
-    for g in range(GROUPS):
-        for h in range(g * GH, (g + 1) * GH):
-            time_backward(h)
-        spread(c_b, group_cols[g], put_sc[g], 4, g)
-        if g == 0:
+    def time_back_group(g, carry):
+        for n in range(GH):
+            time_backward(g * GH + n)
+        spread(c_b, group_cols(g), put_sc(g), 4, g)
+
+        @pl.when(g == 0)
+        def _():
             forward(whole, put_out, 7, 0)
-        else:
-            forward(group_cols[g - 1], put_sc[g - 1], 4, g - 1)
-
+
+        @pl.when(g > 0)
+        def _():
+            forward(group_cols(g - 1), put_sc(g - 1), 4, g - 1)
+
+        return carry
+
+    lax.fori_loop(0, GROUPS, time_back_group, 0)
     spread(a_b, whole, put_tqg, 5, 0)
 
     await_bytes(b_b, a2a_ss.at[7])
 
     def space_backward(h):
-        hs = pl.ds(h * HD, HD)
+        hs = rows(h * HD, HD)
         weights = pw[h]
         cot = sc_r[:, hs]
         key = k_s[:, hs]
@@ -309,16 +337,16 @@
         dv_x[:, hs] = dv[ROWS:].astype(B16)
 
     def backward_group(g):
-        cols = pl.ds(g * GC, GC)
+        cols = group_cols(g)
         await_bytes(sc_r.at[:, cols], sc_rs.at[g])
-        for h in range(g * GH, (g + 1) * GH):
-            space_backward(h)
+        for n in range(GH):
+            space_backward(g * GH + n)
         send(dk_x.at[:, cols], dk_r.at[:, cols], x_ss, x_rs.at[0, g], other)
         send(dv_x.at[:, cols], dv_r.at[:, cols], x_ss, x_rs.at[1, g], other)
 
     await_bytes(t_r, t_rs)
     tt[...] = t_r[...].T
-    forward(group_cols[GROUPS - 1], put_sc[GROUPS - 1], 4, GROUPS - 1)
+    forward(group_cols(GROUPS - 1), put_sc(GROUPS - 1), 4, GROUPS - 1)
     await_bytes(u_half(y_m, 1), y_rs.at[3])
     await_bytes(u_half(y_p, 0), y_rs.at[2])
     y_f = (y + 2) % YS
@@ -337,79 +365,97 @@
         wgf[k, 0] = part[:, :COLS]
         wgf[k, 1] = part[:, COLS:]
 
-    def pair_sum(k):
+    def pair_sum(k, along_z):
         await_bytes(crecv.at[k], c_rs.at[k])
         rsend[k] = (wgf[k, core] + crecv[k].astype(F32)).astype(B16)
         for step in range(1, 4):
             xd = (x + step) % 4
             send(rsend.at[k, rows(xd * SUB, SUB)], ra.at[x, k], r_ss.at[0], r_rs.at[0], dev(xd, y, zh, zl, core))
-        if k > 0:
+        if along_z:
             zhd, zld = chip(k)
             send(rsend.at[k, pl.ds(SIDE, SIDE)], rb.at[z], r_ss.at[1], r_rs.at[1], dev(x, y, zhd, zld, core))
 
-    order = (1, 2, 3, 0)
-    for n, k in enumerate(order):
+    def weight_step(n, carry):
+        k = (n + 1) % 4
         weight_part(k)
         csend[k] = wgf[k, 1 - core].astype(B16)
         send(csend.at[k], crecv.at[k], c_ss, c_rs.at[k], other)
-        if n > 0:
-            pair_sum(order[n - 1])
-    pair_sum(0)
+
+        @pl.when(n > 0)
+        def _():
+            pair_sum(n, True)
+
+        return carry
+
+    lax.fori_loop(0, 4, weight_step, 0)
+    pair_sum(0, False)
     spread(d_b, whole, put_tkg, 6, 0)
     forward(whole, put_tqg, 5, 0)
-    backward_group(0)
-
-    for k in range(4):
-        ra[x, k] = rsend[k, rows(x * SUB, SUB)]
-    rb[z] = rsend[0, SIDE:]
-    await_bytes(ra.at[pl.ds(0, 3)], r_rs.at[0])
-    for k in range(4):
-        total = ra[0, k].astype(F32)
+    def first_stage():
+        for k in range(4):
+            ra[x, k] = rsend[k, rows(x * SUB, SUB)]
+        rb[z] = rsend[0, SIDE:]
+        await_bytes(ra.at[pl.ds(0, 3)], r_rs.at[0])
+        for k in range(4):
+            total = ra[0, k].astype(F32)
+            for n in range(1, 4):
+                total = total + ra[n, k].astype(F32)
+            sa[k] = total.astype(B16)
+            if k > 0:
+                zhd, zld = chip(k)
+                send(sa.at[k], ra2.at[z], r_ss.at[2], r_rs.at[2], dev(x, y, zhd, zld, core))
+        ra2[z] = sa[0]
+        await_bytes(rb.at[pl.ds(0, 3)], r_rs.at[1])
+        total = rb[0].astype(F32)
         for n in range(1, 4):
-            total = total + ra[n, k].astype(F32)
-        sa[k] = total.astype(B16)
-        if k > 0:
-            zhd, zld = chip(k)
-            send(sa.at[k], ra2.at[z], r_ss.at[2], r_rs.at[2], dev(x, y, zhd, zld, core))
-    ra2[z] = sa[0]
-    await_bytes(rb.at[pl.ds(0, 3)], r_rs.at[1])
-    total = rb[0].astype(F32)
-    for n in range(1, 4):
-        total = total + rb[n].astype(F32)
-    sb[...] = total.astype(B16)
-    for step in range(1, 4):
-        xd = (x + step) % 4
-        send(sb.at[rows(xd * SUB, SUB)], rb2.at[x], r_ss.at[3], r_rs.at[3], dev(xd, y, zh, zl, core))
-    rb2[x] = sb[rows(x * SUB, SUB)]
-    backward_group(1)
-
-    for part, (held, n) in enumerate(((ra2, 2), (rb2, 3))):
-        await_bytes(held.at[pl.ds(0, 3)], r_rs.at[n])
-        total = held[0].astype(F32)
-        for k in range(1, 4):
-            total = total + held[k].astype(F32)
-        red[part * SUB:(part + 1) * SUB] = total.astype(B16)
-    out_cols = rows(((zh * 2 + zl) * 2 + core) * COLS, COLS)
+            total = total + rb[n].astype(F32)
+        sb[...] = total.astype(B16)
+        for step in range(1, 4):
+            xd = (x + step) % 4
+            send(sb.at[rows(xd * SUB, SUB)], rb2.at[x], r_ss.at[3], r_rs.at[3], dev(xd, y, zh, zl, core))
+        rb2[x] = sb[rows(x * SUB, SUB)]
+
+    out_cols = rows((z * 2 + core) * COLS, COLS)
     zh_own, core_own = y // 2, y % 2
-    for k in range(8):
-        yd, zld = (y + k // 2) % YS, (zl + k) % 2
-        mine = (yd == y) & (zh_own == zh) & (zld == zl) & (core_own == core)
-
-        @pl.when(mine)
+
+    def second_stage():
+        for part, (held, n) in enumerate(((ra2, 2), (rb2, 3))):
+            await_bytes(held.at[pl.ds(0, 3)], r_rs.at[n])
+            total = held[0].astype(F32)
+            for k in range(1, 4):
+                total = total + held[k].astype(F32)
+            red[part * SUB:(part + 1) * SUB] = total.astype(B16)
+        for k in range(8):
+            yd, zld = (y + k // 2) % YS, (zl + k) % 2
+            mine = (yd == y) & (zh_own == zh) & (zld == zl) & (core_own == core)
+
+            @pl.when(mine)
+            def _():
+                local(red, g_r.at[:, out_cols], g_rs)
+
+            @pl.when(jnp.logical_not(mine))
+            def _():
+                send(red, g_r.at[:, out_cols], g_ss.at[k], g_rs, dev(x, yd, zh_own, zld, core_own))
+
+    def backward_step(g, carry):
+        backward_group(g)
+
+        @pl.when(g == 0)
         def _():
-            local(red, g_r.at[:, out_cols], g_rs)
-
-        @pl.when(jnp.logical_not(mine))
+            first_stage()
+
+        @pl.when(g == 1)
         def _():
-            send(red, g_r.at[:, out_cols], g_ss.at[k], g_rs, dev(x, yd, zh_own, zld, core_own))
-
-    forward(whole, put_tkg, 6, 0)
-    backward_group(2)
-    backward_group(3)
+            second_stage()
+            forward(whole, put_tkg, 6, 0)
+
+        return carry
+
+    lax.fori_loop(0, GROUPS, backward_step, 0)
 
     local(b_b, sqg_o.at[0], out_s.at[0])
     for g in range(GROUPS):
-        cols = pl.ds(g * GC, GC)
+        cols = group_cols(g)
         await_bytes(dk_r.at[:, cols], x_rs.at[0, g])
         await_bytes(dv_r.at[:, cols], x_rs.at[1, g])
     await_bytes(dk_x, x_ss)

time: 121 us -> 121 us (level)
  no operation moved by 1% of the time
where the time goes in v5:
time: 121 us
  Pallas kernels  121 us (100%)
    pallas_call x1, Pallas kernels, local(): pl.pallas_call(kernel, out_shape=(unit,) * 5 + (jax.ShapeDtypeStruct((OUT...  117 us
    pallas_call x1, Pallas kernels, local(): pl.pallas_call(store, out_shape=(unit,) * 5 + (jax.ShapeDtypeStruct((OUT_...  3.74 us

profile of v5, /device:TPU:1, one launch (start us, length us, event | category | flops | bytes accessed | tf_op | source)
XLA Modules:
  0.0 121.1 jit_solution(13966684319364213556)
XLA Ops:
  0.6 116.8 %shard_map.127 = (bf16[1,256,1536]{2,1,0:T(8,128)(2,1)}, bf16[1,256,1536]{2,1,0:T(8,128)(2,1)}, bf16[1,256,1536]{2,1,0:T(8,128)(2,1)}, bf16[1,256,1536]{2,1,0:T(...) custom-call(bf16[1,256,1536]{2,1,0:T(8,128)(2,1)} %qs.1, bf16[1,256,1536]{2,1,0:T(8,128)(2,1)} %ks.1, ...), custom_call_target="tpu_custom_call" | custom-call | flops 8000000000 | bytes 20000000 | tf_op jit(solution)/shard_map/pallas_call | solution.py:531
  117.4 3.7 %shard_map.128 = (bf16[1,256,1536]{2,1,0:T(8,128)(2,1)}, bf16[1,256,1536]{2,1,0:T(8,128)(2,1)}, bf16[1,256,1536]{2,1,0:T(8,128)(2,1)}, bf16[1,256,1536]{2,1,0:T(...) custom-call(bf16[1,256,1536]{2,1,0:T(8,128)(2,1)} %get-tuple-element.12.a, ...), custom_call_target="tpu_custom_call" | custom-call | tf_op jit(solution)/shard_map/pallas_call | solution.py:561

commit v6 on v5

--- a/solution.py
+++ b/solution.py
@@ -66,6 +66,10 @@
             src_ref=src, dst_ref=dst, send_sem=ss, recv_sem=rs, device_id=to, device_id_type=MESH
         ).start()
 
+    def send_pieces(src, dst, count, step, ss, rs, to):
+        for i in range(0, count, step):
+            send(src.at[pl.ds(i, step)], dst.at[pl.ds(i, step)], ss, rs, to)
+
     def await_bytes(ref, sem):
         pltpu.make_async_copy(ref, ref, sem).wait()
 
@@ -143,12 +147,17 @@
     y_up = dev(x, (y + 1) % YS, zh, zl, core)
     y_dn = dev(x, (y + 3) % YS, zh, zl, core)
 
-    half = ROWS // 2
+    cut = 160
     own_k, far_k = pl.ds(0, ROWS), pl.ds(ROWS, ROWS)
     own_u = pl.ds(pl.multiple_of(y * ROWS, ROWS), ROWS)
 
     def u_half(owner, part):
-        return u_s.at[pl.ds(pl.multiple_of(owner * ROWS + part * half, half), half)]
+        start, size = (0, cut) if part == 0 else (cut, ROWS - cut)
+        return u_s.at[pl.ds(pl.multiple_of(owner * ROWS + start, PIX), size)]
+
+    def send_upstream(owner, part, n, to):
+        ref = u_half(owner, part)
+        send_pieces(ref, ref, ref.shape[0], PIX, y_ss.at[n], y_rs.at[n], to)
 
     loads = (
         (ks.at[0], k_s.at[own_k]), (vs.at[0], v_s.at[own_k]), (qt.at[0], b_b), (kt.at[0], d_b),
@@ -160,18 +169,18 @@
         local(w.at[pl.ds(i * WROWS, WROWS)], w_s.at[pl.ds(i * WROWS, WROWS)], ld.at[6 + i])
 
     await_bytes(k_s.at[own_k], ld.at[0])
-    send(k_s.at[own_k], k_s.at[far_k], kv_ss.at[0], kv_rs.at[0], other)
+    send_pieces(k_s.at[own_k], k_s.at[far_k], ROWS, PIX, kv_ss.at[0], kv_rs.at[0], other)
     await_bytes(v_s.at[own_k], ld.at[1])
-    send(v_s.at[own_k], v_s.at[far_k], kv_ss.at[1], kv_rs.at[1], other)
+    send_pieces(v_s.at[own_k], v_s.at[far_k], ROWS, PIX, kv_ss.at[1], kv_rs.at[1], other)
     await_bytes(b_b, ld.at[2])
     spread(b_b, whole, put_tq, 0, 0)
     await_bytes(u_s.at[own_u], ld.at[4])
-    send(u_half(y, 0), u_half(y, 0), y_ss.at[0], y_rs.at[0], y_up)
-    send(u_half(y, 1), u_half(y, 1), y_ss.at[1], y_rs.at[1], y_dn)
+    send_upstream(y, 0, 0, y_up)
+    send_upstream(y, 1, 1, y_dn)
     await_bytes(d_b, ld.at[3])
     spread(d_b, whole, put_tk, 1, 0)
-    send(u_half(y, 0), u_half(y, 0), y_ss.at[2], y_rs.at[2], y_dn)
-    send(u_half(y, 1), u_half(y, 1), y_ss.at[3], y_rs.at[3], y_up)
+    send_upstream(y, 0, 2, y_dn)
+    send_upstream(y, 1, 3, y_up)
 
     key_row = lax.broadcasted_iota(jnp.int32, (P_SIZE, NT), 0)
     key_tile = jnp.where(
@@ -220,6 +229,12 @@
     forward(whole, put_tk, 1, 0)
     spread(c_b, whole, put_oc, 2, 0)
 
+    y_m, y_p = (y + 3) % YS, (y + 1) % YS
+    await_bytes(u_half(y_m, 0), y_rs.at[0])
+    send_upstream(y_m, 0, 4, y_up)
+    await_bytes(u_half(y_p, 1), y_rs.at[1])
+    send_upstream(y_p, 1, 5, y_dn)
+
     await_bytes(tq_r, a2a_rs.at[0])
     await_bytes(tk_r, a2a_rs.at[1])
 
@@ -252,12 +267,6 @@
         return carry
 
     lax.fori_loop(0, GROUPS, forward_space, 0)
-
-    y_m, y_p = (y + 3) % YS, (y + 1) % YS
-    await_bytes(u_half(y_m, 0), y_rs.at[0])
-    send(u_half(y_m, 0), u_half(y_m, 0), y_ss.at[4], y_rs.at[4], y_up)
-    await_bytes(u_half(y_p, 1), y_rs.at[1])
-    send(u_half(y_p, 1), u_half(y_p, 1), y_ss.at[5], y_rs.at[5], y_dn)
 
     await_bytes(b_b, a2a_ss.at[0])
     def apply_group(g, carry):
@@ -341,8 +350,8 @@
         await_bytes(sc_r.at[:, cols], sc_rs.at[g])
         for n in range(GH):
             space_backward(g * GH + n)
-        send(dk_x.at[:, cols], dk_r.at[:, cols], x_ss, x_rs.at[0, g], other)
-        send(dv_x.at[:, cols], dv_r.at[:, cols], x_ss, x_rs.at[1, g], other)
+        send_pieces(dk_x.at[:, cols], dk_r.at[:, cols], ROWS, 64, x_ss, x_rs.at[0, g], other)
+        send_pieces(dv_x.at[:, cols], dv_r.at[:, cols], ROWS, 64, x_ss, x_rs.at[1, g], other)
 
     await_bytes(t_r, t_rs)
     tt[...] = t_r[...].T
@@ -379,7 +388,7 @@
         k = (n + 1) % 4
         weight_part(k)
         csend[k] = wgf[k, 1 - core].astype(B16)
-        send(csend.at[k], crecv.at[k], c_ss, c_rs.at[k], other)
+        send_pieces(csend.at[k], crecv.at[k], BLOCK, OUT_ROWS, c_ss, c_rs.at[k], other)
 
         @pl.when(n > 0)
         def _():
@@ -391,6 +400,7 @@
     pair_sum(0, False)
     spread(d_b, whole, put_tkg, 6, 0)
     forward(whole, put_tqg, 5, 0)
+
     def first_stage():
         for k in range(4):
             ra[x, k] = rsend[k, rows(x * SUB, SUB)]
@@ -472,8 +482,8 @@
 
     await_bytes(k_s.at[own_k], kv_ss.at[0])
     await_bytes(v_s.at[own_k], kv_ss.at[1])
-    for i in range(6):
-        await_bytes(u_half(0, 0), y_ss.at[i])
+    for i, part in enumerate((0, 1, 0, 1, 0, 1)):
+        await_bytes(u_half(0, part), y_ss.at[i])
     await_bytes(c_b, a2a_ss.at[4])
     await_bytes(a_b, a2a_ss.at[5])
     await_bytes(d_b, a2a_ss.at[6])

time: 121 us -> 124 us (1.025)
    pallas_call x1, Pallas kernels: 117 us -> 119 us  [local(): pl.pallas_call(kernel, out_shape=(unit,) * 5 + (jax.ShapeDtypeStruct((OUT...]
where the time goes in v6:
time: 124 us; the launch traced here: 123 us
  Pallas kernels  122 us (98%)
    pallas_call x1, Pallas kernels, local(): pl.pallas_call(kernel, out_shape=(unit,) * 5 + (jax.ShapeDtypeStruct((OUT...  119 us
    pallas_call x1, Pallas kernels, local(): pl.pallas_call(store, out_shape=(unit,) * 5 + (jax.ShapeDtypeStruct((OUT_...  3.74 us

profile of v6, /device:TPU:1, one launch (start us, length us, event | category | flops | bytes accessed | tf_op | source)
XLA Modules:
  0.0 123.1 jit_solution(11508648474054933770)
XLA Ops:
  0.6 118.7 %shard_map.127 = (bf16[1,256,1536]{2,1,0:T(8,128)(2,1)}, bf16[1,256,1536]{2,1,0:T(8,128)(2,1)}, bf16[1,256,1536]{2,1,0:T(8,128)(2,1)}, bf16[1,256,1536]{2,1,0:T(...) custom-call(bf16[1,256,1536]{2,1,0:T(8,128)(2,1)} %qs.1, bf16[1,256,1536]{2,1,0:T(8,128)(2,1)} %ks.1, ...), custom_call_target="tpu_custom_call" | custom-call | flops 8000000000 | bytes 20000000 | tf_op jit(solution)/shard_map/pallas_call | solution.py:541
  119.3 3.7 %shard_map.128 = (bf16[1,256,1536]{2,1,0:T(8,128)(2,1)}, bf16[1,256,1536]{2,1,0:T(8,128)(2,1)}, bf16[1,256,1536]{2,1,0:T(8,128)(2,1)}, bf16[1,256,1536]{2,1,0:T(...) custom-call(bf16[1,256,1536]{2,1,0:T(8,128)(2,1)} %get-tuple-element.12.a, ...), custom_call_target="tpu_custom_call" | custom-call | tf_op jit(solution)/shard_map/pallas_call | solution.py:571

commit v7 on v5

--- a/solution.py
+++ b/solution.py
@@ -24,6 +24,8 @@
 OUT_ROWS = 96
 SUB = OUT_ROWS // 2
 SIDE = BLOCK // 2
+LONG = 32
+SHORT = SUB - LONG
 GROUPS = 4
 GH = HEADS // GROUPS
 GC = GH * HD
@@ -47,10 +49,10 @@
     qs, ks, vs, qt, kt, up, w, mask,
     sqg_o, skg_o, svg_o, tqg_o, tkg_o, wg_o,
     q_s, k_s, v_s, w_s, u_s, tq_r, tk_r, so_r, oc_r, sc_r, t_r,
-    a_b, b_b, c_b, d_b, pw, tw, bias, tbias, tt, wgf, csend, crecv, rsend, ra, rb, ra2, rb2, sa, sb, red,
+    a_b, b_b, c_b, d_b, pw, tw, bias, tbias, tt, wgf, csend, crecv, rsend, ra, rb, fx_up, fx_dn, fz, ra2, rb2, sa, sb, red,
     dk_f, dv_f, dk_x, dv_x, dk_r, dv_r, hop, t_f, tqg_r, tkg_r, g_r,
     ld, kv_ss, kv_rs, y_ss, y_rs, a2a_ss, a2a_rs, so_rs, sc_rs, t_rs, hop_ss, hop_rs,
-    c_ss, c_rs, r_ss, r_rs, g_ss, g_rs, x_ss, x_rs, out_s,
+    c_ss, c_rs, r_ss, r_rs, fx_rs, fz_rs, g_ss, g_rs, x_ss, x_rs, out_s,
 ):
     dp = lax.axis_index("dp")
     seq = lax.axis_index("seq")
@@ -365,50 +367,65 @@
         wgf[k, 0] = part[:, :COLS]
         wgf[k, 1] = part[:, COLS:]
 
-    def pair_sum(k, along_z):
+    x_up, x_dn = dev((x + 1) % 4, y, zh, zl, core), dev((x + 3) % 4, y, zh, zl, core)
+    z_up, z_dn = dev(x, y, *chip(1), core), dev(x, y, *chip(3), core)
+
+    def piece(step, start, size):
+        return pl.ds(pl.multiple_of((x + step) % 4 * SUB + start, BAND), size)
+
+    def pair_sum(k):
         await_bytes(crecv.at[k], c_rs.at[k])
         rsend[k] = (wgf[k, core] + crecv[k].astype(F32)).astype(B16)
-        for step in range(1, 4):
-            xd = (x + step) % 4
-            send(rsend.at[k, rows(xd * SUB, SUB)], ra.at[x, k], r_ss.at[0], r_rs.at[0], dev(xd, y, zh, zl, core))
-        if along_z:
-            zhd, zld = chip(k)
-            send(rsend.at[k, pl.ds(SIDE, SIDE)], rb.at[z], r_ss.at[1], r_rs.at[1], dev(x, y, zhd, zld, core))
-
-    def weight_step(n, carry):
-        k = (n + 1) % 4
+        send(rsend.at[k, piece(2, 0, LONG)], fx_up.at[k], r_ss.at[4], fx_rs.at[0, k], x_up)
+        send(rsend.at[k, piece(2, LONG, SHORT)], fx_dn.at[k], r_ss.at[4], fx_rs.at[1, k], x_dn)
+        if k == 2:
+            send(rsend.at[k, pl.ds(SIDE, OUT_ROWS)], fz.at[0], r_ss.at[5], fz_rs.at[0], z_up)
+            send(rsend.at[k, pl.ds(SIDE + OUT_ROWS, OUT_ROWS)], fz.at[1], r_ss.at[5], fz_rs.at[1], z_dn)
+
+    def add_to(k, where, part):
+        rsend[k, where] = (rsend[k, where].astype(F32) + part.astype(F32)).astype(B16)
+
+    def pass_on(k):
+        await_bytes(fx_up.at[k], fx_rs.at[0, k])
+        add_to(k, piece(1, 0, LONG), fx_up[k])
+        send(rsend.at[k, piece(1, 0, SUB)], ra.at[0, k], r_ss.at[0], r_rs.at[0], x_up)
+        await_bytes(fx_dn.at[k], fx_rs.at[1, k])
+        add_to(k, piece(3, LONG, SHORT), fx_dn[k])
+        send(rsend.at[k, piece(3, 0, SUB)], ra.at[1, k], r_ss.at[0], r_rs.at[0], x_dn)
+        if k == 1:
+            await_bytes(fz.at[0], fz_rs.at[0])
+            add_to(k, pl.ds(SIDE, OUT_ROWS), fz[0])
+            send(rsend.at[k, pl.ds(SIDE, SIDE)], rb.at[0], r_ss.at[1], r_rs.at[1], z_up)
+        if k == 3:
+            await_bytes(fz.at[1], fz_rs.at[1])
+            add_to(k, pl.ds(SIDE + OUT_ROWS, OUT_ROWS), fz[1])
+            send(rsend.at[k, pl.ds(SIDE, SIDE)], rb.at[1], r_ss.at[1], r_rs.at[1], z_dn)
+
+    order = (2, 1, 3, 0)
+    for n, k in enumerate(order):
         weight_part(k)
         csend[k] = wgf[k, 1 - core].astype(B16)
         send(csend.at[k], crecv.at[k], c_ss, c_rs.at[k], other)
-
-        @pl.when(n > 0)
-        def _():
-            pair_sum(n, True)
-
-        return carry
-
-    lax.fori_loop(0, 4, weight_step, 0)
-    pair_sum(0, False)
+        if n > 0:
+            pair_sum(order[n - 1])
+        if n > 1:
+            pass_on(order[n - 2])
+    pair_sum(order[3])
+    pass_on(order[2])
+    pass_on(order[3])
     spread(d_b, whole, put_tkg, 6, 0)
     forward(whole, put_tqg, 5, 0)
     def first_stage():
+        await_bytes(ra, r_rs.at[0])
         for k in range(4):
-            ra[x, k] = rsend[k, rows(x * SUB, SUB)]
-        rb[z] = rsend[0, SIDE:]
-        await_bytes(ra.at[pl.ds(0, 3)], r_rs.at[0])
-        for k in range(4):
-            total = ra[0, k].astype(F32)
-            for n in range(1, 4):
-                total = total + ra[n, k].astype(F32)
+            total = ra[0, k].astype(F32) + ra[1, k].astype(F32) + rsend[k, piece(0, 0, SUB)].astype(F32)
             sa[k] = total.astype(B16)
             if k > 0:
                 zhd, zld = chip(k)
                 send(sa.at[k], ra2.at[z], r_ss.at[2], r_rs.at[2], dev(x, y, zhd, zld, core))
         ra2[z] = sa[0]
-        await_bytes(rb.at[pl.ds(0, 3)], r_rs.at[1])
-        total = rb[0].astype(F32)
-        for n in range(1, 4):
-            total = total + rb[n].astype(F32)
+        await_bytes(rb, r_rs.at[1])
+        total = rb[0].astype(F32) + rb[1].astype(F32) + rsend[0, SIDE:].astype(F32)
         sb[...] = total.astype(B16)
         for step in range(1, 4):
             xd = (x + step) % 4
@@ -480,8 +497,8 @@
     for unit in range(8):
         await_bytes(hop.at[unit], hop_ss.at[unit])
     await_bytes(csend, c_ss)
-    for n, held in enumerate((ra, rb, ra2, rb2)):
-        await_bytes(held.at[pl.ds(0, 3)], r_ss.at[n])
+    for n, held in enumerate((ra, rb, ra2.at[pl.ds(0, 3)], rb2.at[pl.ds(0, 3)], ra.at[0], rb.at[0])):
+        await_bytes(held, r_ss.at[n])
     for k in range(8):
         yd, zld = (y + k // 2) % YS, (zl + k) % 2
         mine = (yd == y) & (zh_own == zh) & (zld == zl) & (core_own == core)
@@ -541,15 +558,16 @@
             vm((P_SIZE, ROWS), F32), vm((GROUP, GROUP), F32),
             vm((BLOCK, YS * ROWS), B16), vm((4, 2, BLOCK, COLS), F32),
             vm((4, BLOCK, COLS), B16), vm((4, BLOCK, COLS), B16),
-            vm((4, BLOCK, COLS), B16), vm((4, 4, SUB, COLS), B16), vm((4, SIDE, COLS), B16),
+            vm((4, BLOCK, COLS), B16), vm((2, 4, SUB, COLS), B16), vm((2, SIDE, COLS), B16),
+            vm((4, LONG, COLS), B16), vm((4, SHORT, COLS), B16), vm((2, OUT_ROWS, COLS), B16),
             vm((4, SUB, COLS), B16), vm((4, SUB, COLS), B16), vm((4, SUB, COLS), B16),
             vm((SIDE, COLS), B16), vm((OUT_ROWS, COLS), B16),
             vm((ROWS, HH), F32), vm((ROWS, HH), F32), own, own, own, own,
             vm((8, 2 * PIX, HH), B16), vm((GROUPS, ROWS, GC), F32),
             own, own, vm((OUT_ROWS, D), B16),
             dma((6 + WCH,)), dma((2,)), dma((2,)), dma((6,)), dma((6,)), dma((8,)), dma((7,)),
-            dma((GROUPS,)), dma((GROUPS,)), dma, dma((8,)), dma((8, GROUPS)), dma, dma((4,)), dma((4,)), dma((4,)),
-            dma((8,)), dma, dma, dma((2, GROUPS)), dma((6,)),
+            dma((GROUPS,)), dma((GROUPS,)), dma, dma((8,)), dma((8, GROUPS)), dma, dma((4,)), dma((6,)), dma((4,)),
+            dma((2, 4)), dma((2,)), dma((8,)), dma, dma, dma((2, GROUPS)), dma((6,)),
         ],
         compiler_params=pltpu.CompilerParams(
             has_side_effects=True, vmem_limit_bytes=62 * 1024 * 1024

time: 121 us -> 122 us (level)
  no operation moved by 1% of the time
where the time goes in v7:
time: 122 us
  Pallas kernels  121 us (99%)
    pallas_call x1, Pallas kernels, local(): pl.pallas_call(kernel, out_shape=(unit,) * 5 + (jax.ShapeDtypeStruct((OUT...  117 us
    pallas_call x1, Pallas kernels, local(): pl.pallas_call(store, out_shape=(unit,) * 5 + (jax.ShapeDtypeStruct((OUT_...  3.74 us

profile of v7, /device:TPU:1, one launch (start us, length us, event | category | flops | bytes accessed | tf_op | source)
XLA Modules:
  0.0 121.7 jit_solution(13452900189351656997)
XLA Ops:
  0.6 117.3 %shard_map.127 = (bf16[1,256,1536]{2,1,0:T(8,128)(2,1)}, bf16[1,256,1536]{2,1,0:T(8,128)(2,1)}, bf16[1,256,1536]{2,1,0:T(8,128)(2,1)}, bf16[1,256,1536]{2,1,0:T(...) custom-call(bf16[1,256,1536]{2,1,0:T(8,128)(2,1)} %qs.1, bf16[1,256,1536]{2,1,0:T(8,128)(2,1)} %ks.1, ...), custom_call_target="tpu_custom_call" | custom-call | flops 8000000000 | bytes 20000000 | tf_op jit(solution)/shard_map/pallas_call | solution.py:548
  118.0 3.7 %shard_map.128 = (bf16[1,256,1536]{2,1,0:T(8,128)(2,1)}, bf16[1,256,1536]{2,1,0:T(8,128)(2,1)}, bf16[1,256,1536]{2,1,0:T(8,128)(2,1)}, bf16[1,256,1536]{2,1,0:T(...) custom-call(bf16[1,256,1536]{2,1,0:T(8,128)(2,1)} %get-tuple-element.12.a, ...), custom_call_target="tpu_custom_call" | custom-call | tf_op jit(solution)/shard_map/pallas_call | solution.py:579

commit v8 on v5

--- a/solution.py
+++ b/solution.py
@@ -143,12 +143,13 @@
     y_up = dev(x, (y + 1) % YS, zh, zl, core)
     y_dn = dev(x, (y + 3) % YS, zh, zl, core)
 
-    half = ROWS // 2
+    cut = 160
     own_k, far_k = pl.ds(0, ROWS), pl.ds(ROWS, ROWS)
     own_u = pl.ds(pl.multiple_of(y * ROWS, ROWS), ROWS)
 
     def u_half(owner, part):
-        return u_s.at[pl.ds(pl.multiple_of(owner * ROWS + part * half, half), half)]
+        start, size = (0, cut) if part == 0 else (cut, ROWS - cut)
+        return u_s.at[pl.ds(pl.multiple_of(owner * ROWS + start, PIX), size)]
 
     loads = (
         (ks.at[0], k_s.at[own_k]), (vs.at[0], v_s.at[own_k]), (qt.at[0], b_b), (kt.at[0], d_b),
@@ -220,6 +221,12 @@
     forward(whole, put_tk, 1, 0)
     spread(c_b, whole, put_oc, 2, 0)
 
+    y_m, y_p = (y + 3) % YS, (y + 1) % YS
+    await_bytes(u_half(y_m, 0), y_rs.at[0])
+    send(u_half(y_m, 0), u_half(y_m, 0), y_ss.at[4], y_rs.at[4], y_up)
+    await_bytes(u_half(y_p, 1), y_rs.at[1])
+    send(u_half(y_p, 1), u_half(y_p, 1), y_ss.at[5], y_rs.at[5], y_dn)
+
     await_bytes(tq_r, a2a_rs.at[0])
     await_bytes(tk_r, a2a_rs.at[1])
 
@@ -252,12 +259,6 @@
         return carry
 
     lax.fori_loop(0, GROUPS, forward_space, 0)
-
-    y_m, y_p = (y + 3) % YS, (y + 1) % YS
-    await_bytes(u_half(y_m, 0), y_rs.at[0])
-    send(u_half(y_m, 0), u_half(y_m, 0), y_ss.at[4], y_rs.at[4], y_up)
-    await_bytes(u_half(y_p, 1), y_rs.at[1])
-    send(u_half(y_p, 1), u_half(y_p, 1), y_ss.at[5], y_rs.at[5], y_dn)
 
     await_bytes(b_b, a2a_ss.at[0])
     def apply_group(g, carry):
@@ -309,14 +310,15 @@
         def _():
             forward(whole, put_out, 7, 0)
 
-        @pl.when(g > 0)
-        def _():
-            forward(group_cols(g - 1), put_sc(g - 1), 4, g - 1)
-
+        return carry
+
+    def forward_cot(g, carry):
+        forward(group_cols(g), put_sc(g), 4, g)
         return carry
 
     lax.fori_loop(0, GROUPS, time_back_group, 0)
     spread(a_b, whole, put_tqg, 5, 0)
+    lax.fori_loop(0, 2, forward_cot, 0)
 
     await_bytes(b_b, a2a_ss.at[7])
 
@@ -346,7 +348,6 @@
 
     await_bytes(t_r, t_rs)
     tt[...] = t_r[...].T
-    forward(group_cols(GROUPS - 1), put_sc(GROUPS - 1), 4, GROUPS - 1)
     await_bytes(u_half(y_m, 1), y_rs.at[3])
     await_bytes(u_half(y_p, 0), y_rs.at[2])
     y_f = (y + 2) % YS
@@ -390,7 +391,8 @@
     lax.fori_loop(0, 4, weight_step, 0)
     pair_sum(0, False)
     spread(d_b, whole, put_tkg, 6, 0)
-    forward(whole, put_tqg, 5, 0)
+    lax.fori_loop(2, GROUPS, forward_cot, 0)
+
     def first_stage():
         for k in range(4):
             ra[x, k] = rsend[k, rows(x * SUB, SUB)]
@@ -447,6 +449,7 @@
         @pl.when(g == 1)
         def _():
             second_stage()
+            forward(whole, put_tqg, 5, 0)
             forward(whole, put_tkg, 6, 0)
 
         return carry
@@ -472,8 +475,8 @@
 
     await_bytes(k_s.at[own_k], kv_ss.at[0])
     await_bytes(v_s.at[own_k], kv_ss.at[1])
-    for i in range(6):
-        await_bytes(u_half(0, 0), y_ss.at[i])
+    for i, part in enumerate((0, 1, 0, 1, 0, 1)):
+        await_bytes(u_half(0, part), y_ss.at[i])
     await_bytes(c_b, a2a_ss.at[4])
     await_bytes(a_b, a2a_ss.at[5])
     await_bytes(d_b, a2a_ss.at[6])

time: 121 us -> 123 us (1.017)
    pallas_call x1, Pallas kernels: 117 us -> 118 us  [local(): pl.pallas_call(kernel, out_shape=(unit,) * 5 + (jax.ShapeDtypeStruct((OUT...]
where the time goes in v8:
time: 123 us; the launch traced here: 122 us
  Pallas kernels  122 us (99%)
    pallas_call x1, Pallas kernels, local(): pl.pallas_call(kernel, out_shape=(unit,) * 5 + (jax.ShapeDtypeStruct((OUT...  118 us
    pallas_call x1, Pallas kernels, local(): pl.pallas_call(store, out_shape=(unit,) * 5 + (jax.ShapeDtypeStruct((OUT_...  3.74 us

profile of v8, /device:TPU:1, one launch (start us, length us, event | category | flops | bytes accessed | tf_op | source)
XLA Modules:
  0.0 122.4 jit_solution(2136190462108723949)
XLA Ops:
  0.6 118.0 %shard_map.127 = (bf16[1,256,1536]{2,1,0:T(8,128)(2,1)}, bf16[1,256,1536]{2,1,0:T(8,128)(2,1)}, bf16[1,256,1536]{2,1,0:T(8,128)(2,1)}, bf16[1,256,1536]{2,1,0:T(...) custom-call(bf16[1,256,1536]{2,1,0:T(8,128)(2,1)} %qs.1, bf16[1,256,1536]{2,1,0:T(8,128)(2,1)} %ks.1, ...), custom_call_target="tpu_custom_call" | custom-call | flops 8000000000 | bytes 20000000 | tf_op jit(solution)/shard_map/pallas_call | solution.py:534
  118.6 3.7 %shard_map.128 = (bf16[1,256,1536]{2,1,0:T(8,128)(2,1)}, bf16[1,256,1536]{2,1,0:T(8,128)(2,1)}, bf16[1,256,1536]{2,1,0:T(8,128)(2,1)}, bf16[1,256,1536]{2,1,0:T(...) custom-call(bf16[1,256,1536]{2,1,0:T(8,128)(2,1)} %get-tuple-element.12.a, ...), custom_call_target="tpu_custom_call" | custom-call | tf_op jit(solution)/shard_map/pallas_call | solution.py:564

commit v9 on v8

--- a/solution.py
+++ b/solution.py
@@ -143,7 +143,7 @@
     y_up = dev(x, (y + 1) % YS, zh, zl, core)
     y_dn = dev(x, (y + 3) % YS, zh, zl, core)
 
-    cut = 160
+    cut = 96
     own_k, far_k = pl.ds(0, ROWS), pl.ds(ROWS, ROWS)
     own_u = pl.ds(pl.multiple_of(y * ROWS, ROWS), ROWS)
 

time: 123 us -> 124 us (level)
    pallas_call x1, Pallas kernels: 118 us -> 119 us  [local(): pl.pallas_call(kernel, out_shape=(unit,) * 5 + (jax.ShapeDtypeStruct((OUT...]
where the time goes in v9:
time: 124 us
  Pallas kernels  123 us (99%)
    pallas_call x1, Pallas kernels, local(): pl.pallas_call(kernel, out_shape=(unit,) * 5 + (jax.ShapeDtypeStruct((OUT...  119 us
    pallas_call x1, Pallas kernels, local(): pl.pallas_call(store, out_shape=(unit,) * 5 + (jax.ShapeDtypeStruct((OUT_...  3.74 us

profile of v9, /device:TPU:1, one launch (start us, length us, event | category | flops | bytes accessed | tf_op | source)
XLA Modules:
  0.0 123.9 jit_solution(16487959969397382129)
XLA Ops:
  0.6 119.5 %shard_map.127 = (bf16[1,256,1536]{2,1,0:T(8,128)(2,1)}, bf16[1,256,1536]{2,1,0:T(8,128)(2,1)}, bf16[1,256,1536]{2,1,0:T(8,128)(2,1)}, bf16[1,256,1536]{2,1,0:T(...) custom-call(bf16[1,256,1536]{2,1,0:T(8,128)(2,1)} %qs.1, bf16[1,256,1536]{2,1,0:T(8,128)(2,1)} %ks.1, ...), custom_call_target="tpu_custom_call" | custom-call | flops 8000000000 | bytes 20000000 | tf_op jit(solution)/shard_map/pallas_call | solution.py:534
  120.1 3.7 %shard_map.128 = (bf16[1,256,1536]{2,1,0:T(8,128)(2,1)}, bf16[1,256,1536]{2,1,0:T(8,128)(2,1)}, bf16[1,256,1536]{2,1,0:T(8,128)(2,1)}, bf16[1,256,1536]{2,1,0:T(...) custom-call(bf16[1,256,1536]{2,1,0:T(8,128)(2,1)} %get-tuple-element.12.a, ...), custom_call_target="tpu_custom_call" | custom-call | tf_op jit(solution)/shard_map/pallas_call | solution.py:564

commit v10 on v5

--- a/solution.py
+++ b/solution.py
@@ -344,9 +344,16 @@
         send(dk_x.at[:, cols], dk_r.at[:, cols], x_ss, x_rs.at[0, g], other)
         send(dv_x.at[:, cols], dv_r.at[:, cols], x_ss, x_rs.at[1, g], other)
 
+    def backward_step(g, carry):
+        backward_group(g)
+        return carry
+
+    forward(group_cols(GROUPS - 1), put_sc(GROUPS - 1), 4, GROUPS - 1)
+    lax.fori_loop(0, 2, backward_step, 0)
+    spread(d_b, whole, put_tkg, 6, 0)
+
     await_bytes(t_r, t_rs)
     tt[...] = t_r[...].T
-    forward(group_cols(GROUPS - 1), put_sc(GROUPS - 1), 4, GROUPS - 1)
     await_bytes(u_half(y_m, 1), y_rs.at[3])
     await_bytes(u_half(y_p, 0), y_rs.at[2])
     y_f = (y + 2) % YS
@@ -389,8 +396,7 @@
 
     lax.fori_loop(0, 4, weight_step, 0)
     pair_sum(0, False)
-    spread(d_b, whole, put_tkg, 6, 0)
-    forward(whole, put_tqg, 5, 0)
+
     def first_stage():
         for k in range(4):
             ra[x, k] = rsend[k, rows(x * SUB, SUB)]
@@ -437,21 +443,11 @@
             def _():
                 send(red, g_r.at[:, out_cols], g_ss.at[k], g_rs, dev(x, yd, zh_own, zld, core_own))
 
-    def backward_step(g, carry):
-        backward_group(g)
-
-        @pl.when(g == 0)
-        def _():
-            first_stage()
-
-        @pl.when(g == 1)
-        def _():
-            second_stage()
-            forward(whole, put_tkg, 6, 0)
-
-        return carry
-
-    lax.fori_loop(0, GROUPS, backward_step, 0)
+    first_stage()
+    second_stage()
+    forward(whole, put_tqg, 5, 0)
+    forward(whole, put_tkg, 6, 0)
+    lax.fori_loop(2, GROUPS, backward_step, 0)
 
     local(b_b, sqg_o.at[0], out_s.at[0])
     for g in range(GROUPS):

time: 121 us -> 122 us (level)
  no operation moved by 1% of the time
where the time goes in v10:
time: 122 us; the launch traced here: 121 us
  Pallas kernels  121 us (99%)
    pallas_call x1, Pallas kernels, local(): pl.pallas_call(kernel, out_shape=(unit,) * 5 + (jax.ShapeDtypeStruct((OUT...  117 us
    pallas_call x1, Pallas kernels, local(): pl.pallas_call(store, out_shape=(unit,) * 5 + (jax.ShapeDtypeStruct((OUT_...  3.74 us

profile of v10, /device:TPU:1, one launch (start us, length us, event | category | flops | bytes accessed | tf_op | source)
XLA Modules:
  0.0 121.4 jit_solution(11917591192833690899)
XLA Ops:
  0.6 117.0 %shard_map.127 = (bf16[1,256,1536]{2,1,0:T(8,128)(2,1)}, bf16[1,256,1536]{2,1,0:T(8,128)(2,1)}, bf16[1,256,1536]{2,1,0:T(8,128)(2,1)}, bf16[1,256,1536]{2,1,0:T(...) custom-call(bf16[1,256,1536]{2,1,0:T(8,128)(2,1)} %qs.1, bf16[1,256,1536]{2,1,0:T(8,128)(2,1)} %ks.1, ...), custom_call_target="tpu_custom_call" | custom-call | flops 8000000000 | bytes 20000000 | tf_op jit(solution)/shard_map/pallas_call | solution.py:527
  117.7 3.7 %shard_map.128 = (bf16[1,256,1536]{2,1,0:T(8,128)(2,1)}, bf16[1,256,1536]{2,1,0:T(8,128)(2,1)}, bf16[1,256,1536]{2,1,0:T(8,128)(2,1)}, bf16[1,256,1536]{2,1,0:T(...) custom-call(bf16[1,256,1536]{2,1,0:T(8,128)(2,1)} %get-tuple-element.12.a, ...), custom_call_target="tpu_custom_call" | custom-call | tf_op jit(solution)/shard_map/pallas_call | solution.py:557

commit v11 on v10

--- a/solution.py
+++ b/solution.py
@@ -85,13 +85,12 @@
                     a2a_ss.at[unit], hop_rs.at[unit, part],
                     dev((x + 1 + 2 * side) % 4, y, zd, 1 - zl, core),
                 )
-        for step in (1, 3, 0):
-            xd = (x + step) % 4
-            for zd in range(2):
-                put(
-                    src, rows((xd * 2 + zd) * PIX, PIX), frame * PIX, PIX, a2a_ss.at[unit],
-                    xd, zd, 1 - zl,
-                )
+        for step, turn in ((1, 0), (3, 1), (0, 0), (1, 1), (3, 0), (0, 1)):
+            xd, zd = (x + step) % 4, (zh + turn) % 2
+            put(
+                src, rows((xd * 2 + zd) * PIX, PIX), frame * PIX, PIX, a2a_ss.at[unit],
+                xd, zd, 1 - zl,
+            )
 
     def forward(cols, put, unit, part):
         await_bytes(hop.at[unit, :, cols], hop_rs.at[unit, part])

time: 122 us -> 121 us (level)
  no operation moved by 1% of the time
where the time goes in v11:
time: 121 us; the launch traced here: 120 us
  Pallas kernels  120 us (99%)
    pallas_call x1, Pallas kernels, local(): pl.pallas_call(kernel, out_shape=(unit,) * 5 + (jax.ShapeDtypeStruct((OUT...  116 us
    pallas_call x1, Pallas kernels, local(): pl.pallas_call(store, out_shape=(unit,) * 5 + (jax.ShapeDtypeStruct((OUT_...  3.74 us

profile of v11, /device:TPU:1, one launch (start us, length us, event | category | flops | bytes accessed | tf_op | source)
XLA Modules:
  0.0 120.5 jit_solution(7510677839622077598)
XLA Ops:
  0.6 116.1 %shard_map.127 = (bf16[1,256,1536]{2,1,0:T(8,128)(2,1)}, bf16[1,256,1536]{2,1,0:T(8,128)(2,1)}, bf16[1,256,1536]{2,1,0:T(8,128)(2,1)}, bf16[1,256,1536]{2,1,0:T(...) custom-call(bf16[1,256,1536]{2,1,0:T(8,128)(2,1)} %qs.1, bf16[1,256,1536]{2,1,0:T(8,128)(2,1)} %ks.1, ...), custom_call_target="tpu_custom_call" | custom-call | flops 8000000000 | bytes 20000000 | tf_op jit(solution)/shard_map/pallas_call | solution.py:526
  116.7 3.7 %shard_map.128 = (bf16[1,256,1536]{2,1,0:T(8,128)(2,1)}, bf16[1,256,1536]{2,1,0:T(8,128)(2,1)}, bf16[1,256,1536]{2,1,0:T(8,128)(2,1)}, bf16[1,256,1536]{2,1,0:T(...) custom-call(bf16[1,256,1536]{2,1,0:T(8,128)(2,1)} %get-tuple-element.12.a, ...), custom_call_target="tpu_custom_call" | custom-call | tf_op jit(solution)/shard_map/pallas_call | solution.py:556
